TPU v7x, 32 devices: a whole 2x2x4 slice. The times are simulated.
32 devices in a mesh: ctx: 8 (over y, x, core), tp: 4 (over z).
Axes of the slice: x: 2, y: 2, z: 4, core: 2. Of those that a mesh axis runs over, the one named last changes fastest.
Arguments:
- queries: bfloat16 [2048, 2048], P('ctx', 'tp'), may hold values from -6 to 6
- key_vectors: bfloat16 [2048, 2048], P('ctx', 'tp'), may hold values from -4 to 4
- value_vectors: bfloat16 [2048, 4096], P('ctx', 'tp'), may hold values from -6 to 6
- output_gate: bfloat16 [2048, 4096], P('ctx', 'tp'), may hold values from -6 to 6
- write_rate: float32 [2048, 32], P('ctx', 'tp'), may hold values from 0 to 1, as said below
- log_decay: float32 [2048, 32], P('ctx', 'tp'), may hold values from -1 to 0, as said below
- norm_gain: float32 [128], replicated, may hold values from 0.5 to 2
- out_weight: bfloat16 [4096, 2048], P('tp'), may hold values from -0.09375 to 0.09375
Outputs:
- mixed: bfloat16 [2048, 2048], P(('ctx', 'tp'))
Inputs may be any that keep to these rules, and one draw needn't show every extreme that they name: `write_rate`: write strengths are positive. `log_decay`: log decays are negative.
All inputs are finite; a program needn't handle non-finite values.
Results may differ from a plain program's by a relative error of at most 0.025.
Values may be sent and summed in bfloat16 or wider, within the bound.
A program may use at most 64 MiB of HBM per device.

v0:
```python
import jax
import jax.numpy as jnp
from jax import lax
from jax.sharding import PartitionSpec as P

DK = 128
DV = 128


highest_precision = lax.Precision.HIGHEST


def prefix(value, axis, combine, identity):
    length, index = (lax.axis_size(axis), lax.axis_index(axis))
    everything = jax.tree.map(
        lambda part, kind: lax.all_gather(part.astype(kind), axis),
        value,
        (jnp.bfloat16, jnp.bfloat16),
    )
    start = jax.tree.map(
        lambda part, zero: jnp.broadcast_to(jnp.asarray(zero, part.dtype), part.shape),
        value,
        identity,
    )

    def lap(k, before):
        reached = k < index
        new = combine(
            before, jax.tree.map(lambda part, own: part[k].astype(own.dtype), everything, value)
        )
        return jax.tree.map(lambda a, b: jnp.where(reached, a, b), new, before)

    return lax.fori_loop(0, length, lap, start)


def matmul(left, right):
    return jnp.matmul(left, right, precision=highest_precision)


def flipped(matrix):
    return jnp.swapaxes(matrix, -1, -2)


def unit_rows(source, count_heads, size_head):
    values_f = source.astype(jnp.float32).reshape(source.shape[0], count_heads, size_head)
    return values_f * lax.rsqrt(jnp.sum(values_f * values_f, axis=-1, keepdims=True) + 1e-06)


def to_blocks(source, count, length):
    return jnp.transpose(
        source.reshape(count, length, source.shape[1], source.shape[2]), (0, 2, 1, 3)
    )


def local(
    queries, key_vectors, value_vectors, output_gate, write_rate, log_decay, norm_gain, out_weight
):
    tokens_here = queries.shape[0]
    key_heads = queries.shape[1] // DK
    value_heads = value_vectors.shape[1] // DV
    sharing = value_heads // key_heads
    length = min(64, tokens_here)
    count = tokens_here // length
    query_blocks = to_blocks(
        jnp.repeat(unit_rows(queries, key_heads, DK), sharing, axis=1), count, length
    )
    key_blocks = to_blocks(
        jnp.repeat(unit_rows(key_vectors, key_heads, DK), sharing, axis=1), count, length
    )
    value_blocks = to_blocks(
        value_vectors.astype(jnp.float32).reshape(tokens_here, value_heads, DV), count, length
    )
    rate_blocks = jnp.transpose(write_rate.reshape(count, length, value_heads), (0, 2, 1))[
        ..., None
    ]
    decay_sums = jnp.cumsum(
        jnp.transpose(log_decay.reshape(count, length, value_heads), (0, 2, 1)), axis=-1
    )
    closing = decay_sums[..., -1:]
    positions = jnp.arange(length)
    inclusive = positions[:, None] >= positions[None, :]
    strict = positions[:, None] > positions[None, :]
    spread = decay_sums[..., :, None] - decay_sums[..., None, :]
    ratios = jnp.where(inclusive, jnp.exp(jnp.where(inclusive, spread, 0.0)), 0.0)
    key_gram = matmul(key_blocks, flipped(key_blocks))
    lower = jnp.where(strict, rate_blocks * key_gram * ratios, 0.0)
    identity = jnp.eye(length, dtype=jnp.float32)
    inverse = identity - lower
    power = lower
    reach = 1
    while reach < length - 1:
        power = matmul(power, power)
        inverse = matmul(inverse, identity + power)
        reach = 2 * reach + 1
    fresh = matmul(inverse, rate_blocks * value_blocks)
    erase = matmul(inverse, rate_blocks * jnp.exp(decay_sums)[..., None] * key_blocks)
    scores = ratios * matmul(query_blocks, flipped(key_blocks))
    read_query = jnp.exp(decay_sums)[..., None] * query_blocks
    write_key = jnp.exp(closing - decay_sums)[..., None] * key_blocks
    fade = jnp.exp(closing)[..., None]
    eye_key = jnp.broadcast_to(jnp.eye(DK, dtype=jnp.float32), (value_heads, DK, DK))
    empty_state = jnp.zeros((value_heads, DK, DV), jnp.float32)
    per_block = (fresh, erase, scores, read_query, write_key, fade)

    def summarize(carry, block):
        transit, held = carry
        fresh_b, erase_b, score_b, read_b, write_b, fade_b = block
        moved = fade_b * transit - matmul(flipped(write_b), matmul(erase_b, transit))
        delta = fresh_b - matmul(erase_b, held)
        return ((moved, fade_b * held + matmul(flipped(write_b), delta)), None)

    (transit, held), _ = lax.scan(summarize, (eye_key, empty_state), per_block)

    def compose(earlier, later):
        return (matmul(later[0], earlier[0]), matmul(later[0], earlier[1]) + later[1])

    _, start_state = prefix((transit, held), "ctx", compose, (eye_key, empty_state))

    def advance(current, block):
        fresh_b, erase_b, score_b, read_b, write_b, fade_b = block
        delta = fresh_b - matmul(erase_b, current)
        produced = matmul(read_b, current) + matmul(score_b, delta)
        return (fade_b * current + matmul(flipped(write_b), delta), produced)

    _, core_blocks = lax.scan(advance, start_state, per_block)
    attention_core = jnp.transpose(core_blocks, (0, 2, 1, 3)).reshape(tokens_here, value_heads, DV)
    square_mean = jnp.mean(attention_core * attention_core, axis=-1, keepdims=True)
    gate_full = output_gate.astype(jnp.float32).reshape(tokens_here, value_heads, DV)
    normed = attention_core * lax.rsqrt(square_mean + 1e-06) * norm_gain * jax.nn.silu(gate_full)
    normed = normed.astype(jnp.bfloat16).reshape(tokens_here, value_heads * DV)
    return lax.psum_scatter(
        jnp.dot(normed, out_weight, preferred_element_type=jnp.float32).astype(jnp.bfloat16),
        "tp",
        scatter_dimension=0,
        tiled=True,
    )


def solution(mesh):
    placed = (
        P("ctx", "tp"),
        P("ctx", "tp"),
        P("ctx", "tp"),
        P("ctx", "tp"),
        P("ctx", "tp"),
        P("ctx", "tp"),
        P(),
        P("tp", None),
    )
    return jax.shard_map(
        local, mesh=mesh, in_specs=placed, out_specs=P(("ctx", "tp"), None), check_vma=False
    )
```

profile of v0, /device:TPU:4, one launch (start us, length us, event | category | flops | bytes accessed | tf_op | source)
XLA Modules:
  0.0 186.7 jit_solution(9912683888037385327)
XLA Ops:
  6.6 1.1 reshape.89
  8.7 0.9 reduce_window_sum.11
  9.8 1.9 %fusion.43 = f32[4,8,64,64]{3,2,1,0:T(8,128)S(1)} fusion(f32[4,8,64,128]{3,2,0,1:T(8,128)S(1)} %bitcast.166, f32[4,8,128,64]{2,3,0,1:T(8,128)S(1)} %bitcast.167, f32[4,8,64]{2,1,0:T(8,128)S(1)} %reduce_window_sum.11, f32[4,8,64]{2,1,0:T(8,128)S(1)} %bitcast.179, pred[64,64]{1,0:T(8,128)(4,1)S(1)} %get-tuple-element.343, ...), kind=kOutput, calls=%fused_computation.56 | convolution fusion | flops 202113024 | bytes 2646016 | tf_op jit(solution)/shard_map/dot_general | solution.py:37
  11.7 1.2 fusion.80
  12.9 1.2 fusion.81
  14.1 1.2 fusion.61
  15.3 1.2 fusion.82
  16.5 1.2 fusion.59
  17.7 1.2 fusion.83
  18.8 1.2 fusion.57
  20.0 1.2 convolution_add_fusion.4
  21.2 1.4 fusion.55
  23.0 1.2 fusion.84
  24.2 2.3 %fusion.49 = f32[4,8,64,128]{3,2,1,0:T(8,128)} fusion(f32[4,8,64,64]{3,2,1,0:T(8,128)S(1)} %fusion.84, f32[4,64,8,128]{3,2,1,0:T(8,128)S(1)} %bitcast.172, f32[4,8,64]{2,1,0:T(8,128)S(1)} %bitcast.180), kind=kOutput, calls=%fused_computation.66 | convolution fusion | flops 201588736 | bytes 2629632 | tf_op jit(solution)/shard_map/dot_general | solution.py:37
  27.1 1.2 fusion.52
  28.5 17.7 %while.40 = (s32[]{:T(128)}, f32[8,128,128]{2,1,0:T(8,128)S(1)}, f32[8,128,128]{2,1,0:T(8,128)S(1)}, f32[4,8,1,1]{1,3,2,0:T(1,128)S(1)}, f32[4,8,64,128]{3,2,1,0...) while((s32[]{:T(128)}, f32[8,128,128]{2,1,0:T(8,128)S(1)}, ...), condition=%wide.region_3.4_spmd.clone, body=%wide.region_2.0_spmd.clone.sunk | while | flops 403505152 | bytes 5507256 | solution.py:112
  28.5 1.5 convolution_subtract_fusion.8
  30.1 1.1 convolution_add_fusion.8
  31.8 1.1 convolution_subtract_fusion.7
  32.9 1.5 convolution_subtract_fusion.8
  34.5 1.1 convolution_add_fusion.8
  36.2 1.1 convolution_subtract_fusion.7
  37.4 1.5 convolution_subtract_fusion.8
  38.9 1.1 convolution_add_fusion.8
  40.7 1.1 convolution_subtract_fusion.7
  41.8 1.5 convolution_subtract_fusion.8
  43.4 1.1 convolution_add_fusion.8
  45.1 1.1 convolution_subtract_fusion.7
  46.3 0.7 convert_element_type.54
  47.1 0.8 convert_element_type.55
  49.2 1.3 broadcast_multiply_fusion
  50.6 2.8 %convolution_multiply_fusion = f32[4,8,64,64]{3,2,1,0:T(8,128)} fusion(f32[4,8,64,128]{3,2,0,1:T(8,128)S(1)} %bitcast.171, f32[4,8,128,64]{2,3,0,1:T(8,128)S(1)} %bitcast.169, f32[4,8,64]{2,1,0:T(8,128)S(1)} %reduce_window_sum.11, pred[64,64]{1,0:T(8,128)(4,1)S(1)} %get-tuple-element.343), kind=kOutput, calls=%fused_computation.52 | convolution fusion | flops 201850880 | bytes 2633728 | tf_op jit(solution)/shard_map/dot_general | solution.py:37
  53.4 22.9 %all-gather.5.cloned.1.call-done = bf16[64,128,128]{2,1,0:T(8,128)(2,1)} async-done(((bf16[8,128,128]{2,1,0:T(8,128)(2,1)}), bf16[64,128,128]{2,1,0:T(8,128)(2,1)}) %all-gather.5.cloned.1.call-update) | async-done | bytes 2097168 | tf_op jit(solution)/shard_map/all_gather | solution.py:16
  76.2 29.8 %all-gather.7.cloned.1.call-done = bf16[64,128,128]{2,1,0:T(8,128)(2,1)} async-done(((bf16[8,128,128]{2,1,0:T(8,128)(2,1)}), bf16[64,128,128]{2,1,0:T(8,128)(2,1)}) %all-gather.7.cloned.1.call-update) | async-done | bytes 2097168 | tf_op jit(solution)/shard_map/all_gather | solution.py:16
  106.0 12.7 %while.41 = (s32[]{:T(128)}, f32[8,128,128]{2,1,0:T(8,128)S(1)}, s32[]{:T(128)}, bf16[8,8,128,128]{3,2,1,0:T(8,128)(2,1)}, bf16[8,8,128,128]{3,2,1,0:T(8,128)(2,1)}, /*index=5*/s32[]{:T(128)}, s32[]{:T(128)}) while((s32[]{:T(128)}, f32[8,128,128]{2,1,0:T(8,128)S(1)}, s32[]{:T(128)}, bf16[8,8,128,128]{3,2,1,0:T(8,128)(2,1)}, ...), condition=%wide.region_5.6_spmd.clone, body=%wide.region_4.5_spmd.clone.sunk | while | flops 201981952 | bytes 3148383 | solution.py:33
  106.1 1.5 fusion.157
  107.7 1.5 fusion.157
  109.3 1.5 fusion.157
  110.9 1.5 fusion.157
  112.5 1.5 fusion.157
  114.0 1.5 fusion.157
  115.6 1.5 fusion.157
  117.2 1.5 fusion.157
  118.8 25.4 %while.39 = (s32[]{:T(128)}, f32[8,128,128]{2,1,0:T(8,128)S(1)}, f32[4,8,64,128]{3,2,1,0:T(8,128)}, f32[4,8,1,1]{1,3,2,0:T(1,128)S(1)}, f32[4,8,64,128]{3,2,1,0:...) while((s32[]{:T(128)}, f32[8,128,128]{2,1,0:T(8,128)S(1)}, ...), condition=%wide.region_8.9_spmd, body=%wide.region_7.8_spmd.sunk | while | flops 352714752 | bytes 4983981 | solution.py:125
  118.8 1.6 convolution_subtract_fusion.6
  120.4 1.6 fusion.143
  121.9 2.0 %fusion.144 = f32[4,8,64,128]{3,2,1,0:T(8,128)} fusion(f32[4,8,64,128]{3,2,1,0:T(8,128)} %get-tuple-element.534, s32[]{:T(128)} %get-tuple-element.532, f32[8,64,128]{2,1,0:T(8,128)S(1)} %fusion.143, f32[8,64,128]{2,1,0:T(8,128)S(1)} %convolution_subtract_fusion.6, f32[4,8,64,64]{3,2,1,0:T(8,128)} %get-tuple-element.550), kind=kOutput, calls=%fused_computation.3.clone.1 | convolution fusion | flops 50397184 | bytes 1049600 | tf_op jit(solution)/shard_map/while/body/eval_jaxpr/dot_general | solution.py:37
  124.0 1.1 convolution_add_fusion.7
  125.1 1.6 convolution_subtract_fusion.6
  126.7 1.6 fusion.143
  128.3 2.1 %fusion.144 = f32[4,8,64,128]{3,2,1,0:T(8,128)} fusion(f32[4,8,64,128]{3,2,1,0:T(8,128)} %get-tuple-element.534, s32[]{:T(128)} %get-tuple-element.532, f32[8,64,128]{2,1,0:T(8,128)S(1)} %fusion.143, f32[8,64,128]{2,1,0:T(8,128)S(1)} %convolution_subtract_fusion.6, f32[4,8,64,64]{3,2,1,0:T(8,128)} %get-tuple-element.550), kind=kOutput, calls=%fused_computation.3.clone.1 | convolution fusion | flops 50397184 | bytes 1049600 | tf_op jit(solution)/shard_map/while/body/eval_jaxpr/dot_general | solution.py:37
  130.3 1.1 convolution_add_fusion.7
  131.5 1.6 convolution_subtract_fusion.6
  133.0 1.6 fusion.143
  134.6 2.1 %fusion.144 = f32[4,8,64,128]{3,2,1,0:T(8,128)} fusion(f32[4,8,64,128]{3,2,1,0:T(8,128)} %get-tuple-element.534, s32[]{:T(128)} %get-tuple-element.532, f32[8,64,128]{2,1,0:T(8,128)S(1)} %fusion.143, f32[8,64,128]{2,1,0:T(8,128)S(1)} %convolution_subtract_fusion.6, f32[4,8,64,64]{3,2,1,0:T(8,128)} %get-tuple-element.550), kind=kOutput, calls=%fused_computation.3.clone.1 | convolution fusion | flops 50397184 | bytes 1049600 | tf_op jit(solution)/shard_map/while/body/eval_jaxpr/dot_general | solution.py:37
  136.7 1.1 convolution_add_fusion.7
  137.8 1.6 convolution_subtract_fusion.6
  139.4 1.6 fusion.143
  141.0 2.1 %fusion.144 = f32[4,8,64,128]{3,2,1,0:T(8,128)} fusion(f32[4,8,64,128]{3,2,1,0:T(8,128)} %get-tuple-element.534, s32[]{:T(128)} %get-tuple-element.532, f32[8,64,128]{2,1,0:T(8,128)S(1)} %fusion.143, f32[8,64,128]{2,1,0:T(8,128)S(1)} %convolution_subtract_fusion.6, f32[4,8,64,64]{3,2,1,0:T(8,128)} %get-tuple-element.550), kind=kOutput, calls=%fused_computation.3.clone.1 | convolution fusion | flops 50397184 | bytes 1049600 | tf_op jit(solution)/shard_map/while/body/eval_jaxpr/dot_general | solution.py:37
  143.1 1.1 convolution_add_fusion.7
  144.2 1.6 multiply_reduce_fusion
  145.9 1.8 copy.69
  148.1 4.7 %convolution_convert_fusion = bf16[256,2048]{1,0:T(8,128)(2,1)} fusion(bf16[1024,2048]{1,0:T(8,128)(2,1)} %param.21, bf16[256,1024]{1,0:T(8,128)(2,1)S(1)} %copy-done.7, f32[32,8,8,128]{3,2,1,0:T(8,128)S(1)} %bitcast.174, f32[32,8,8,128]{3,2,1,0:T(8,128)S(1)} %bitcast.175, f32[1024]{0:T(1024)S(1)} %broadcast_bitcast_fusion), kind=kOutput, calls=%fused_computation.51 | convolution fusion | flops 1076625408 | bytes 7868416 | tf_op jit(solution)/shard_map/dot_general | solution.py:132
  152.8 27.4 %reduce-scatter.2.cloned.1.call-done = bf16[64,2048]{1,0:T(8,128)(2,1)} async-done(((bf16[256,2048]{1,0:T(8,128)(2,1)}), bf16[64,2048]{1,0:T(8,128)(2,1)}) %reduce-scatter.2.cloned.1.call-update) | async-done | bytes 262160 | tf_op jit(solution)/shard_map/reduce_scatter | solution.py:131
  (77 shorter events, 6.9 us)
Async XLA Ops:
  6.5 42.6 %copy-start = (f32[128]{0:T(128)S(1)}, f32[128]{0:T(128)}, u32[]{:S(2)}) copy-start(f32[128]{0:T(128)} %param.20) | copy-start | bytes 1540
  6.5 2.0 %copy-start.5 = (f32[256,8]{0,1:T(8,128)S(1)}, f32[256,8]{0,1:T(8,128)}, u32[]{:S(2)}) copy-start(f32[256,8]{0,1:T(8,128)} %param.19) | copy-start | bytes 24580
  6.5 2.1 %copy-start.6 = (f32[256,8]{0,1:T(8,128)S(1)}, f32[256,8]{0,1:T(8,128)}, u32[]{:S(2)}) copy-start(f32[256,8]{0,1:T(8,128)} %param.18) | copy-start | bytes 24580
  6.5 69.7 %all-gather.5.cloned.1.call-start = ((), (), s32[]{:S(2)}) async-start(), calls=%async_computation.2 | async-start | bytes 2359296 | tf_op jit(solution)/shard_map/all_gather | solution.py:16
  9.8 16.7 %copy-start.1 = (f32[256,4,2,128]{3,0,2,1:T(8,128)}, f32[256,4,2,128]{3,0,2,1:T(8,128)S(1)}, u32[]{:S(2)}) copy-start(f32[256,4,2,128]{3,0,2,1:T(8,128)S(1)} %broadcast_in_dim.61) | copy-start | bytes 3145732
  21.2 1.4 copy-start.3
  46.2 1.9 %copy-start.4 = (bf16[256,512]{1,0:T(8,128)(2,1)S(1)}, bf16[256,512]{1,0:T(8,128)(2,1)}, u32[]{:S(2)}) copy-start(bf16[256,512]{1,0:T(8,128)(2,1)} %param.14) | copy-start | bytes 786436
  47.0 59.0 %all-gather.7.cloned.1.call-start = ((), (), s32[]{:S(2)}) async-start(), calls=%async_computation.3 | async-start | bytes 2359296 | tf_op jit(solution)/shard_map/all_gather | solution.py:16
  47.9 132.3 %reduce-scatter.2.cloned.1.call-start = ((), (), s32[]{:S(2)}) async-start(), calls=%async_computation.1 | async-start | bytes 1310720 | tf_op jit(solution)/shard_map/reduce_scatter | solution.py:131
  49.1 1.4 copy-start.2
  144.2 3.9 %copy-start.7 = (bf16[256,1024]{1,0:T(8,128)(2,1)S(1)}, bf16[256,1024]{1,0:T(8,128)(2,1)}, u32[]{:S(2)}) copy-start(bf16[256,1024]{1,0:T(8,128)(2,1)} %param.17) | copy-start | bytes 1572868
Sparse Core Ops, SparseCore 0:
  47.1 29.0 all-gather.4
  78.1 27.8 all-gather.6
  153.0 27.1 reduce-scatter.1
where the time goes:
time: 189 us; the launch traced here: 187 us
  waiting for transfers between devices  80.1 us (42%)
  matrix products  79.7 us (42%)
  between operations  13.5 us (7%)
  other arithmetic  7.6 us (4%)
  local copies, waits for them, and re-layouts  4.82 us (3%)
    dot_general x54, matrix products, matmul(): return jnp.matmul(left, right, precision=highest_precision)  75.1 us
    all_gather x2, waiting for transfers between devices, prefix(): lax.all_gather(part.astype(kind), axis)  52.7 us
    reduce_scatter x1, waiting for transfers between devices, local(): lax.psum_scatter(jnp.dot(normed, out_weight, preferred_element_type=jnp.f...  27.4 us
    dot_general x1, matrix products, local(): jnp.dot(normed, out_weight, preferred_element_type=jnp.float32)  4.69 us
  transfers between devices with their start and end apart: 3, of which 3 were waited for; matrix products, arithmetic and copies ran while one was open for 3% of the time, Pallas kernels for 0%

commit v1 on v0

v1 whole, which is shorter than its diff:
```python
import functools

import jax
import jax.numpy as jnp
from jax import lax
from jax.experimental import pallas as pl
from jax.experimental.pallas import tpu as pltpu
from jax.sharding import PartitionSpec as P

DK = 128
DV = 128
MESH = pl.DeviceIdType.MESH
f32, bf16 = jnp.float32, jnp.bfloat16


def mm(left, right):
    return jnp.dot(left, right, preferred_element_type=f32)


def mm_rows(left, right):
    return lax.dot_general(left, right, (((1,), (1,)), ((), ())), preferred_element_type=f32)


def mm_cols(left, right):
    return lax.dot_general(left, right, (((0,), (0,)), ((), ())), preferred_element_type=f32)


def unit_lower_inverse(lower, row, col):
    size = lower.shape[0]
    eye = row == col

    def between(step):
        return (row // (2 * step) == col // (2 * step)) & (row // step != col // step)

    inverse = jnp.where(eye, 1.0, jnp.where(between(1), -lower, 0.0))
    step = 2
    while step < size:
        coupling = jnp.where(between(step), lower, 0.0).astype(bf16)
        rounded = inverse.astype(bf16)
        inverse = inverse - mm(rounded, mm(coupling, rounded).astype(bf16))
        step *= 2
    rounded = inverse.astype(bf16)
    high = lower.astype(bf16)
    low = (lower - high.astype(f32)).astype(bf16)
    base = rounded.astype(f32)
    residual = jnp.where(eye, 1.0, 0.0) - base - mm(high, rounded) - mm(low, rounded)
    return base + mm(rounded, residual.astype(bf16))


def summary_kernel(sharing, q_ref, k_ref, v_ref, rate_ref, decay_ref, map_ref, read_ref, own_ref):
    group = pl.program_id(0)
    tokens = q_ref.shape[0]
    half = tokens // 2
    row = lax.broadcasted_iota(jnp.int32, (tokens, tokens), 0)
    col = lax.broadcasted_iota(jnp.int32, (tokens, tokens), 1)
    eye, inclusive, strict = row == col, row >= col, row > col
    half_row = lax.broadcasted_iota(jnp.int32, (half, half), 0)
    half_col = lax.broadcasted_iota(jnp.int32, (half, half), 1)
    key_row = lax.broadcasted_iota(jnp.int32, (DK, DK), 0)
    key_col = lax.broadcasted_iota(jnp.int32, (DK, DK), 1)
    lane = lax.broadcasted_iota(jnp.int32, rate_ref.shape, 1)

    def to_row(column):
        return jnp.sum(jnp.where(eye, column, 0.0), axis=0, keepdims=True)

    def to_col(line):
        return jnp.sum(jnp.where(eye, line, 0.0), axis=1, keepdims=True)

    queries, keys = q_ref[...], k_ref[...]
    queries_f, keys_f = queries.astype(f32), keys.astype(f32)
    query_scale = lax.rsqrt(jnp.sum(queries_f * queries_f, axis=1, keepdims=True) + 1e-06)
    key_scale = lax.rsqrt(jnp.sum(keys_f * keys_f, axis=1, keepdims=True) + 1e-06)
    key_scale_row = to_row(key_scale)
    gram = mm_rows(keys, keys) * key_scale
    reads = mm_rows(queries, keys) * query_scale
    scaled_queries = queries_f * query_scale

    for member in range(sharing):
        head = group * sharing + member
        here = lane == head
        rate = jnp.sum(jnp.where(here, rate_ref[...], 0.0), axis=1, keepdims=True)
        decay = jnp.sum(jnp.where(here, decay_ref[...], 0.0), axis=1, keepdims=True)
        total_row = jnp.sum(jnp.where(row <= col, decay, 0.0), axis=0, keepdims=True)
        total = to_col(total_row)
        rate_row = to_row(rate)
        erase_row = rate_row * jnp.exp(total_row) * key_scale_row
        ratios = jnp.where(inclusive, jnp.exp(jnp.where(inclusive, total - total_row, 0.0)), 0.0)
        ratios = ratios * key_scale_row
        scores = (reads * ratios).astype(bf16)
        lower = jnp.where(strict, rate * gram * ratios, 0.0)
        first = unit_lower_inverse(lower[:half, :half], half_row, half_col)
        second = unit_lower_inverse(lower[half:, half:], half_row, half_col)
        across = mm(lower[half:, :half].astype(bf16), first.astype(bf16))
        across = -mm(second.astype(bf16), across.astype(bf16))
        values = v_ref[:, member * DV : (member + 1) * DV]

        def solved(scale_row, right):
            left_scale, right_scale = scale_row[:, :half], scale_row[:, half:]
            top = mm((first * left_scale).astype(bf16), right[:half])
            bottom = mm((across * left_scale).astype(bf16), right[:half])
            bottom += mm((second * right_scale).astype(bf16), right[half:])
            return jnp.concatenate([top, bottom], axis=0)

        both = jnp.concatenate([solved(erase_row, keys), solved(rate_row, values)], axis=1)
        closing = total[tokens - 1 :, :]
        weight = jnp.exp(closing - total) * key_scale
        summary = mm_cols(keys, (both * weight).astype(bf16))
        fade = jnp.exp(closing)
        moved = jnp.where(key_row == key_col, fade, 0.0) - summary[:, :DK]
        map_ref[member, :, :DK] = moved.astype(bf16)
        map_ref[member, :, DK:] = summary[:, DK:].astype(bf16)
        seen = mm(scores, both.astype(bf16))
        place = slice(member * DV, (member + 1) * DV)
        read_ref[:, place] = (jnp.exp(total) * scaled_queries - seen[:, :DK]).astype(bf16)
        own_ref[:, place] = seen[:, DK:]


def finish_kernel(
    n, groups, map_ref, read_ref, own_ref, gate_ref, gain_ref, weight_hbm, out_ref,
    arrived, leaving, state, normed, weight, part, out_r, out_l, in_r, in_l,
    weight_sem, map_send, map_recv, state_send, state_recv,
    send_r, recv_r, send_l, recv_l,
):
    heads = map_ref.shape[0]
    apart = n // heads
    chunks, _, rows, width = part.shape
    me, spot = lax.axis_index("ctx"), lax.axis_index("tp")
    my_head = me // apart
    owner = lax.rem(me, apart) == 0

    weight_copy = pltpu.make_async_copy(weight_hbm, weight, weight_sem)
    weight_copy.start()

    barrier = pltpu.get_barrier_semaphore()
    for other in range(n):
        @pl.when(me != other)
        def _():
            pl.semaphore_signal(barrier, inc=1, device_id={"ctx": other}, device_id_type=MESH)

    after, before = lax.rem(spot + 1, groups), lax.rem(spot + groups - 1, groups)

    @pl.when(spot > 0)
    def _():
        pl.semaphore_signal(barrier, inc=1, device_id={"tp": before}, device_id_type=MESH)

    @pl.when(spot < groups - 1)
    def _():
        pl.semaphore_signal(barrier, inc=1, device_id={"tp": after}, device_id_type=MESH)

    peers = (spot > 0).astype(jnp.int32) + (spot < groups - 1).astype(jnp.int32)
    pl.semaphore_wait(barrier, n - 1 + peers)

    def map_copy(head, slot, target):
        return pltpu.make_async_remote_copy(
            src_ref=map_ref.at[head], dst_ref=arrived.at[slot],
            send_sem=map_send.at[head], recv_sem=map_recv.at[slot],
            device_id={"ctx": target}, device_id_type=MESH,
        )

    for head in range(heads):
        @pl.when((me != head * apart) & (me < n - 1))
        def _():
            map_copy(head, me, head * apart).start()

    def state_copy(head, target):
        return pltpu.make_async_remote_copy(
            src_ref=leaving.at[target], dst_ref=state.at[head],
            send_sem=state_send.at[target], recv_sem=state_recv.at[head],
            device_id={"ctx": target}, device_id_type=MESH,
        )

    @pl.when(me == 0)
    def _():
        state[...] = jnp.zeros_like(state)

    @pl.when(owner)
    def _():
        arrived[pl.ds(me, 1)] = map_ref[pl.ds(my_head, 1)]
        current = jnp.zeros((DK, DV), f32)
        for step in range(n - 1):
            @pl.when(me != step)
            def _():
                map_copy(0, step, step).wait_recv()

            high = current.astype(bf16)
            low = (current - high.astype(f32)).astype(bf16)
            turned = mm(arrived[step, :, :DK], jnp.concatenate([high, low], axis=1))
            current = turned[:, :DV] + turned[:, DV:] + arrived[step, :, DK:].astype(f32)

            @pl.when(me != step + 1)
            def _():
                leaving[step + 1] = current.astype(bf16)
                state_copy(my_head, step + 1).start()

            @pl.when(me == step + 1)
            def _():
                state[pl.ds(my_head, 1)] = current.astype(bf16)[None]

    gain = gain_ref[...]
    for head in range(heads):
        @pl.when((me > 0) & (me != head * apart))
        def _():
            state_copy(head, 0).wait_recv()

        place = slice(head * DV, (head + 1) * DV)
        core = mm(read_ref[:, place], state[head]) + own_ref[:, place]
        square_mean = jnp.mean(core * core, axis=1, keepdims=True)
        gate = gate_ref[:, place].astype(f32)
        gated = core * lax.rsqrt(square_mean + 1e-06) * gain * (gate / (1.0 + jnp.exp(-gate)))
        normed[:, place] = gated.astype(bf16)

    def right_copy(source, c, target):
        return pltpu.make_async_remote_copy(
            src_ref=source.at[c, target], dst_ref=in_r.at[c, target],
            send_sem=send_r.at[c, target], recv_sem=recv_r.at[c, target],
            device_id={"tp": after}, device_id_type=MESH,
        )

    def left_copy(source, c, target):
        return pltpu.make_async_remote_copy(
            src_ref=source.at[c, target], dst_ref=in_l.at[c, target],
            send_sem=send_l.at[c, target], recv_sem=recv_l.at[c, target],
            device_id={"tp": before}, device_id_type=MESH,
        )

    @pl.when(spot == 0)
    def _():
        in_r[:, 0] = jnp.zeros_like(in_r[:, 0])

    @pl.when(spot == groups - 1)
    def _():
        in_l[:, groups - 1] = jnp.zeros_like(in_l[:, groups - 1])

    weight_copy.wait()
    for c in range(chunks):
        product = mm(normed[...], weight[:, c * width : (c + 1) * width]).astype(bf16)
        part[c] = product.reshape(groups, rows, width)

        @pl.when(spot == 0)
        def _():
            for target in range(groups - 1, 0, -1):
                right_copy(part, c, target).start()

        @pl.when(spot == groups - 1)
        def _():
            for target in range(groups - 1):
                left_copy(part, c, target).start()

    for c in range(chunks):
        def relay(step, carry):
            far = groups - 1 - step

            @pl.when((spot > 0) & (far > spot))
            def _():
                right_copy(part, c, far).wait_recv()
                out_r[c, far] = (in_r[c, far].astype(f32) + part[c, far].astype(f32)).astype(bf16)
                right_copy(out_r, c, far).start()

            @pl.when((spot < groups - 1) & (step < spot))
            def _():
                left_copy(part, c, step).wait_recv()
                out_l[c, step] = (in_l[c, step].astype(f32) + part[c, step].astype(f32)).astype(bf16)
                left_copy(out_l, c, step).start()

            return carry

        lax.fori_loop(0, groups - 1, relay, 0)

    for c in range(chunks):
        @pl.when(spot > 0)
        def _():
            right_copy(part, c, spot).wait_recv()

        @pl.when(spot < groups - 1)
        def _():
            left_copy(part, c, spot).wait_recv()

        mixed = part[c, spot].astype(f32) + in_r[c, spot].astype(f32) + in_l[c, spot].astype(f32)
        out_ref[:, c * width : (c + 1) * width] = mixed.astype(bf16)

    for head in range(heads):
        @pl.when((me != head * apart) & (me < n - 1))
        def _():
            map_copy(head, me, head * apart).wait_send()

    for target in range(1, n):
        @pl.when(owner & (me != target))
        def _():
            state_copy(my_head, target).wait_send()

    for c in range(chunks):
        def drain(target, carry):
            @pl.when(target > spot)
            def _():
                right_copy(part, c, target).wait_send()

            @pl.when(target < spot)
            def _():
                left_copy(part, c, target).wait_send()

            return carry

        lax.fori_loop(0, groups, drain, 0)


def local(n, groups, queries, key_vectors, value_vectors, output_gate, write_rate, log_decay, norm_gain, out_weight):
    tokens = queries.shape[0]
    key_heads = queries.shape[1] // DK
    heads = value_vectors.shape[1] // DV
    sharing = heads // key_heads
    features, model = out_weight.shape
    small = pl.BlockSpec((tokens, heads), lambda g: (0, 0))
    maps, read, own = pl.pallas_call(
        functools.partial(summary_kernel, sharing),
        grid=(key_heads,),
        in_specs=[
            pl.BlockSpec((tokens, DK), lambda g: (0, g)),
            pl.BlockSpec((tokens, DK), lambda g: (0, g)),
            pl.BlockSpec((tokens, sharing * DV), lambda g: (0, g)),
            small,
            small,
        ],
        out_specs=[
            pl.BlockSpec((sharing, DK, DK + DV), lambda g: (g, 0, 0)),
            pl.BlockSpec((tokens, sharing * DV), lambda g: (0, g)),
            pl.BlockSpec((tokens, sharing * DV), lambda g: (0, g)),
        ],
        out_shape=[
            jax.ShapeDtypeStruct((heads, DK, DK + DV), bf16),
            jax.ShapeDtypeStruct((tokens, heads * DV), bf16),
            jax.ShapeDtypeStruct((tokens, heads * DV), f32),
        ],
        compiler_params=pltpu.CompilerParams(vmem_limit_bytes=32 * 2**20),
    )(queries, key_vectors, value_vectors, write_rate, log_decay)

    rows = tokens // groups
    chunks = 4
    width = model // chunks
    piece = pltpu.VMEM((chunks, groups, rows, width), bf16)
    dma = pltpu.SemaphoreType.DMA
    vmem = pl.BlockSpec(memory_space=pltpu.VMEM)
    return pl.pallas_call(
        functools.partial(finish_kernel, n, groups),
        in_specs=[vmem] * 5 + [pl.BlockSpec(memory_space=pl.ANY)],
        out_specs=vmem,
        out_shape=jax.ShapeDtypeStruct((rows, model), bf16),
        scratch_shapes=[
            pltpu.VMEM((n, DK, DK + DV), bf16),
            pltpu.VMEM((n, DK, DV), bf16),
            pltpu.VMEM((heads, DK, DV), bf16),
            pltpu.VMEM((tokens, features), bf16),
            pltpu.VMEM((features, model), bf16),
            piece, piece, piece, piece, piece,
            dma, dma((heads,)), dma((n,)), dma((n,)), dma((heads,)),
            dma((chunks, groups)), dma((chunks, groups)), dma((chunks, groups)), dma((chunks, groups)),
        ],
        compiler_params=pltpu.CompilerParams(
            collective_id=0, has_side_effects=True, vmem_limit_bytes=48 * 2**20
        ),
    )(maps, read, own, output_gate, norm_gain.reshape(1, DV), out_weight)


def solution(mesh):
    placed = (
        P("ctx", "tp"),
        P("ctx", "tp"),
        P("ctx", "tp"),
        P("ctx", "tp"),
        P("ctx", "tp"),
        P("ctx", "tp"),
        P(),
        P("tp", None),
    )
    body = functools.partial(local, mesh.shape["ctx"], mesh.shape["tp"])
    return jax.shard_map(
        body, mesh=mesh, in_specs=placed, out_specs=P(("ctx", "tp"), None), check_vma=False
    )
```

time: 189 us -> 91.8 us (0.49)
  Pallas kernels: 0 us -> 84.2 us
  waiting for transfers between devices: 80.1 us -> 0 us
  matrix products: 79.7 us -> 0 us
  between operations: 13.5 us -> 0.05 us
  other arithmetic: 7.6 us -> 0 us
  local copies, waits for them, and re-layouts: 4.82 us -> 6.97 us
    pallas_call x0 -> x2, Pallas kernels: none -> 84.2 us  [the longest x1 51.6 us: local(): pl.pallas_call(functools.partial(finish_kernel, n, groups), in_specs=[vme...]
    dot_general x55 -> x0, matrix products: 79.7 us -> none  [the longest x54 75.1 us: matmul(): return jnp.matmul(left, right, precision=highest_precision)]
    all_gather x2 -> x0, waiting for transfers between devices: 52.7 us -> none  [prefix(): lax.all_gather(part.astype(kind), axis)]
    reduce_scatter x1 -> x0, waiting for transfers between devices: 27.4 us -> none  [local(): lax.psum_scatter(jnp.dot(normed, out_weight, preferred_element_type=jnp.f...]
    unnamed x18 -> x13, local copies, waits for them, and re-layouts: 0.34 us -> 6.97 us
    mul x4 -> x0, other arithmetic: 2.61 us -> none  [the longest x1 1.34 us: local(): read_query = jnp.exp(decay_sums)[..., None] * query_blocks]
    reduce_sum x3 -> x0, other arithmetic: 2.31 us -> none  [the longest x1 1.62 us: local(): jnp.mean(attention_core * attention_core, axis=-1, keepdims=True)]
  transfers between devices with their start and end apart: 3 -> 0, of which waited for: 3 -> 0; matrix products, arithmetic and copies ran while one was open for 3% -> 0% of each run, Pallas kernels for 0% -> 0%
where the time goes in v1:
time: 91.8 us; the launch traced here: 91.2 us
  Pallas kernels  84.2 us (92%)
  local copies, waits for them, and re-layouts  6.97 us (8%)
    pallas_call x1, Pallas kernels, local(): pl.pallas_call(functools.partial(finish_kernel, n, groups), in_specs=[vme...  51.6 us
    pallas_call x1, Pallas kernels, local(): pl.pallas_call(functools.partial(summary_kernel, sharing), grid=(key_head...  32.6 us
    unnamed x13, local copies, waits for them, and re-layouts  6.97 us

profile of v1, /device:TPU:4, one launch (start us, length us, event | category | flops | bytes accessed | tf_op | source)
XLA Modules:
  0.0 91.2 jit_solution(6110962570451937745)
XLA Ops:
  0.0 0.8 copy.9.rate_ref
  0.8 0.8 copy.10.decay_ref
  1.7 0.0 copy-start.1
  1.7 1.0 %copy-done.1 = bf16[256,1024]{1,0:T(8,128)(2,1)S(1)} copy-done((bf16[256,1024]{1,0:T(8,128)(2,1)S(1)}, bf16[256,1024]{1,0:T(8,128)(2,1)}, u32[]{:S(2)}) %copy-start.1) | copy-done | bytes 524312
  2.7 0.0 copy-start.2
  2.7 0.9 %copy-done.2 = bf16[256,512]{1,0:T(8,128)(2,1)S(1)} copy-done((bf16[256,512]{1,0:T(8,128)(2,1)S(1)}, bf16[256,512]{1,0:T(8,128)(2,1)}, u32[]{:S(2)}) %copy-start.2) | copy-done | bytes 262168
  3.7 0.0 copy-start.3
  3.7 0.9 %copy-done.3 = bf16[256,512]{1,0:T(8,128)(2,1)S(1)} copy-done((bf16[256,512]{1,0:T(8,128)(2,1)S(1)}, bf16[256,512]{1,0:T(8,128)(2,1)}, u32[]{:S(2)}) %copy-start.3) | copy-done | bytes 262168
  4.6 32.6 %shard_map.82 = (bf16[8,128,256]{2,1,0:T(8,128)(2,1)S(1)}, bf16[256,1024]{1,0:T(8,128)(2,1)S(1)}, f32[256,1024]{1,0:T(8,128)S(1)}) custom-call(bf16[256,512]{1,0:T(8,128)(2,1)S(1)} %copy-done.2, bf16[256,512]{1,0:T(8,128)(2,1)S(1)} %copy-done.3, bf16[256,1024]{1,0:T(8,128)(2,1)S(1)} %copy-done.1, f32[256,8]{1,0:T(8,128)S(1)} %copy.9.rate_ref, ...), custom_call_target="tpu_custom_call" | custom-call | tf_op jit(solution)/shard_map/pallas_call | solution.py:313
  37.2 0.0 copy-start
  37.3 1.0 %copy-done = bf16[256,1024]{1,0:T(8,128)(2,1)S(1)} copy-done((bf16[256,1024]{1,0:T(8,128)(2,1)S(1)}, bf16[256,1024]{1,0:T(8,128)(2,1)}, u32[]{:S(2)}) %copy-start) | copy-done | bytes 524312
  38.3 0.0 copy-start.4
  38.3 0.7 copy-done.4
  38.9 51.6 %shard_map.83 = bf16[64,2048]{1,0:T(8,128)(2,1)S(1)} custom-call(bf16[8,128,256]{2,1,0:T(8,128)(2,1)S(1)} %get-tuple-element.8.map_ref, bf16[256,1024]{1,0:T(8,128)(2,1)S(1)} %get-tuple-element.9.read_ref, f32[256,1024]{1,0:T(8,128)S(1)} %get-tuple-element.10.own_ref, bf16[256,1024]{1,0:T(8,128)(2,1)S(1)} %copy-done, f32[1,128]{1,0:T(1,128)S(1)} %bitcast.1, ...), custom_call_target="tpu_custom_call" | custom-call | tf_op jit(solution)/shard_map/pallas_call | solution.py:342
  90.5 0.7 copy.12
Async XLA Ops:
  1.7 1.0 %copy-start.1 = (bf16[256,1024]{1,0:T(8,128)(2,1)S(1)}, bf16[256,1024]{1,0:T(8,128)(2,1)}, u32[]{:S(2)}) copy-start(bf16[256,1024]{1,0:T(8,128)(2,1)} %v_ref.1) | copy-start | bytes 1572868
  2.7 0.9 %copy-start.2 = (bf16[256,512]{1,0:T(8,128)(2,1)S(1)}, bf16[256,512]{1,0:T(8,128)(2,1)}, u32[]{:S(2)}) copy-start(bf16[256,512]{1,0:T(8,128)(2,1)} %q_ref.1) | copy-start | bytes 786436
  3.7 0.9 %copy-start.3 = (bf16[256,512]{1,0:T(8,128)(2,1)S(1)}, bf16[256,512]{1,0:T(8,128)(2,1)}, u32[]{:S(2)}) copy-start(bf16[256,512]{1,0:T(8,128)(2,1)} %k_ref.1) | copy-start | bytes 786436
  37.2 1.0 %copy-start = (bf16[256,1024]{1,0:T(8,128)(2,1)S(1)}, bf16[256,1024]{1,0:T(8,128)(2,1)}, u32[]{:S(2)}) copy-start(bf16[256,1024]{1,0:T(8,128)(2,1)} %gate_ref.1) | copy-start | bytes 1572868
  38.3 0.7 copy-start.4

commit v2 on v1

v2 whole, which is shorter than its diff:
```python
import functools

import jax
import jax.numpy as jnp
from jax import lax
from jax.experimental import pallas as pl
from jax.experimental.pallas import tpu as pltpu
from jax.sharding import PartitionSpec as P

DK = 128
DV = 128
MESH = pl.DeviceIdType.MESH
f32, bf16 = jnp.float32, jnp.bfloat16


def mm(left, right):
    return jnp.dot(left, right, preferred_element_type=f32)


def mm_rows(left, right):
    return lax.dot_general(left, right, (((1,), (1,)), ((), ())), preferred_element_type=f32)


def mm_cols(left, right):
    return lax.dot_general(left, right, (((0,), (0,)), ((), ())), preferred_element_type=f32)


def unit_lower_inverses(lowers):
    size = lowers[0].shape[0]
    row = lax.broadcasted_iota(jnp.int32, (size, size), 0)
    col = lax.broadcasted_iota(jnp.int32, (size, size), 1)
    apart = row ^ col
    eye = jnp.where(row == col, 1.0, 0.0)
    inverses = [eye - jnp.where(apart == 1, lower, 0.0) for lower in lowers]
    step = 2
    while step < size:
        coupling = (apart >= step) & (apart < 2 * step)
        rounded = [inverse.astype(bf16) for inverse in inverses]
        inner = [
            mm(jnp.where(coupling, lower, 0.0).astype(bf16), r).astype(bf16)
            for lower, r in zip(lowers, rounded)
        ]
        inverses = [inverse - mm(r, i) for inverse, r, i in zip(inverses, rounded, inner)]
        step *= 2
    rounded = [inverse.astype(bf16) for inverse in inverses]
    highs = [lower.astype(bf16) for lower in lowers]
    lows = [(lower - high.astype(f32)).astype(bf16) for lower, high in zip(lowers, highs)]
    residuals = [
        (eye - r.astype(f32) - mm(high, r) - mm(low, r)).astype(bf16)
        for high, low, r in zip(highs, lows, rounded)
    ]
    return [r.astype(f32) + mm(r, residual) for r, residual in zip(rounded, residuals)]


def summarize(groups, sharing, q_ref, k_ref, v_ref, rate_ref, decay_ref, map_ref, read_ref, own_ref):
    tokens = q_ref.shape[0]
    half = tokens // 2
    row = lax.broadcasted_iota(jnp.int32, (tokens, tokens), 0)
    col = lax.broadcasted_iota(jnp.int32, (tokens, tokens), 1)
    eye, inclusive, strict = row == col, row >= col, row > col
    key_row = lax.broadcasted_iota(jnp.int32, (DK, DK), 0)
    key_col = lax.broadcasted_iota(jnp.int32, (DK, DK), 1)

    def to_row(column):
        return jnp.sum(jnp.where(eye, column, 0.0), axis=0, keepdims=True)

    def to_col(line):
        return jnp.sum(jnp.where(eye, line, 0.0), axis=1, keepdims=True)

    parts = []
    for group in groups:
        key_place = slice(group * DK, (group + 1) * DK)
        queries, keys = q_ref[:, key_place], k_ref[:, key_place]
        queries_f, keys_f = queries.astype(f32), keys.astype(f32)
        query_scale = lax.rsqrt(jnp.sum(queries_f * queries_f, axis=1, keepdims=True) + 1e-06)
        key_scale = lax.rsqrt(jnp.sum(keys_f * keys_f, axis=1, keepdims=True) + 1e-06)
        key_scale_row = to_row(key_scale)
        gram = mm_rows(keys, keys) * key_scale
        reads = mm_rows(queries, keys) * query_scale
        for member in range(sharing):
            head = group * sharing + member
            rate_row = rate_ref[head : head + 1, :]
            decay_row = decay_ref[head : head + 1, :]
            rate, decay = to_col(rate_row), to_col(decay_row)
            total_row = jnp.sum(jnp.where(row <= col, decay, 0.0), axis=0, keepdims=True)
            total = to_col(total_row)
            erase_row = rate_row * jnp.exp(total_row) * key_scale_row
            ratios = jnp.where(inclusive, jnp.exp(jnp.where(inclusive, total - total_row, 0.0)), 0.0)
            ratios = ratios * key_scale_row
            scores = (reads * ratios).astype(bf16)
            lower = jnp.where(strict, rate * gram * ratios, 0.0)
            read = jnp.exp(total) * query_scale * queries_f
            parts.append((head, keys, key_scale, rate_row, erase_row, total, scores, lower, read))

    inverses = unit_lower_inverses(
        [block for part in parts for block in (part[7][:half, :half], part[7][half:, half:])]
    )
    firsts, seconds = inverses[0::2], inverses[1::2]
    inner = [
        mm(part[7][half:, :half].astype(bf16), first.astype(bf16)).astype(bf16)
        for part, first in zip(parts, firsts)
    ]
    corners = [-mm(second.astype(bf16), i) for second, i in zip(seconds, inner)]

    for part, first, second, corner in zip(parts, firsts, seconds, corners):
        head, keys, key_scale, rate_row, erase_row, total, scores, _, read = part
        place = slice(head * DV, (head + 1) * DV)

        def solved(scale_row, right):
            left_scale, right_scale = scale_row[:, :half], scale_row[:, half:]
            top = mm((first * left_scale).astype(bf16), right[:half])
            bottom = mm((corner * left_scale).astype(bf16), right[:half])
            bottom += mm((second * right_scale).astype(bf16), right[half:])
            return jnp.concatenate([top, bottom], axis=0)

        both = jnp.concatenate([solved(erase_row, keys), solved(rate_row, v_ref[:, place])], axis=1)
        closing = total[tokens - 1 :, :]
        weight = jnp.exp(closing - total) * key_scale
        summary = mm_cols(keys, (both * weight).astype(bf16))
        moved = jnp.where(key_row == key_col, jnp.exp(closing), 0.0) - summary[:, :DK]
        map_ref[head, :, :DK] = moved.astype(bf16)
        map_ref[head, :, DK:] = summary[:, DK:].astype(bf16)
        seen = mm(scores, both.astype(bf16))
        read_ref[:, place] = (read - seen[:, :DK]).astype(bf16)
        own_ref[:, place] = seen[:, DK:]


def layer_kernel(
    n, groups, q_hbm, k_hbm, v_hbm, gate_hbm, rate_hbm, decay_hbm, gain_hbm, weight_hbm, out_ref,
    q_ref, k_ref, v_ref, gate_ref, rate_ref, decay_ref, gain_ref, weight,
    map_ref, read_ref, own_ref, gating,
    arrived, leaving, state, normed, part, out_r, out_l, in_r, in_l,
    load_sem, map_send, map_recv, state_send, state_recv,
    send_r, recv_r, send_l, recv_l,
):
    heads = map_ref.shape[0]
    apart = n // heads
    chunks, _, rows, width = part.shape
    me, spot = lax.axis_index("ctx"), lax.axis_index("tp")
    my_head = me // apart
    owner = lax.rem(me, apart) == 0

    loads = [
        pltpu.make_async_copy(source, target, load_sem.at[i])
        for i, (source, target) in enumerate((
            (k_hbm, k_ref), (q_hbm, q_ref), (rate_hbm, rate_ref), (decay_hbm, decay_ref),
            (v_hbm, v_ref), (gain_hbm, gain_ref), (gate_hbm, gate_ref), (weight_hbm, weight),
        ))
    ]
    for load in loads:
        load.start()

    barrier = pltpu.get_barrier_semaphore()
    for other in range(n):
        @pl.when(me != other)
        def _():
            pl.semaphore_signal(barrier, inc=1, device_id={"ctx": other}, device_id_type=MESH)

    after, before = lax.rem(spot + 1, groups), lax.rem(spot + groups - 1, groups)

    @pl.when(spot > 0)
    def _():
        pl.semaphore_signal(barrier, inc=1, device_id={"tp": before}, device_id_type=MESH)

    @pl.when(spot < groups - 1)
    def _():
        pl.semaphore_signal(barrier, inc=1, device_id={"tp": after}, device_id_type=MESH)

    peers = (spot > 0).astype(jnp.int32) + (spot < groups - 1).astype(jnp.int32)
    def map_copy(head, slot, target):
        return pltpu.make_async_remote_copy(
            src_ref=map_ref.at[head], dst_ref=arrived.at[slot],
            send_sem=map_send.at[head], recv_sem=map_recv.at[slot],
            device_id={"ctx": target}, device_id_type=MESH,
        )

    key_heads = k_ref.shape[1] // DK
    sharing = heads // key_heads
    batch = min(2, key_heads)
    for load in loads[:5]:
        load.wait()

    for start in range(0, key_heads, batch):
        summarize(
            range(start, start + batch), sharing,
            q_ref, k_ref, v_ref, rate_ref, decay_ref, map_ref, read_ref, own_ref,
        )
        if start == 0:
            pl.semaphore_wait(barrier, n - 1 + peers)
        for head in range(start * sharing, (start + batch) * sharing):
            @pl.when((me != head * apart) & (me < n - 1))
            def _():
                map_copy(head, me, head * apart).start()

    for load in loads[5:]:
        load.wait()
    gain = gain_ref[...]
    for head in range(heads):
        place = slice(head * DV, (head + 1) * DV)
        gate = gate_ref[:, place].astype(f32)
        gating[:, place] = gain * (gate / (1.0 + jnp.exp(-gate)))

    def state_copy(head, target):
        return pltpu.make_async_remote_copy(
            src_ref=leaving.at[target], dst_ref=state.at[head],
            send_sem=state_send.at[target], recv_sem=state_recv.at[head],
            device_id={"ctx": target}, device_id_type=MESH,
        )

    @pl.when(me == 0)
    def _():
        state[...] = jnp.zeros_like(state)

    @pl.when(owner)
    def _():
        arrived[pl.ds(me, 1)] = map_ref[pl.ds(my_head, 1)]
        current = jnp.zeros((DK, DV), f32)
        for step in range(n - 1):
            @pl.when(me != step)
            def _():
                map_copy(0, step, step).wait_recv()

            high = current.astype(bf16)
            low = (current - high.astype(f32)).astype(bf16)
            turned = mm(arrived[step, :, :DK], jnp.concatenate([high, low], axis=1))
            current = turned[:, :DV] + turned[:, DV:] + arrived[step, :, DK:].astype(f32)

            @pl.when(me != step + 1)
            def _():
                leaving[step + 1] = current.astype(bf16)
                state_copy(my_head, step + 1).start()

            @pl.when(me == step + 1)
            def _():
                state[pl.ds(my_head, 1)] = current.astype(bf16)[None]

    for head in range(heads):
        @pl.when((me > 0) & (me != head * apart))
        def _():
            state_copy(head, 0).wait_recv()

        place = slice(head * DV, (head + 1) * DV)
        core = mm(read_ref[:, place], state[head]) + own_ref[:, place]
        square_mean = jnp.mean(core * core, axis=1, keepdims=True)
        normed[:, place] = (core * lax.rsqrt(square_mean + 1e-06) * gating[:, place]).astype(bf16)

    def right_copy(source, c, target):
        return pltpu.make_async_remote_copy(
            src_ref=source.at[c, target], dst_ref=in_r.at[c, target],
            send_sem=send_r.at[c, target], recv_sem=recv_r.at[c, target],
            device_id={"tp": after}, device_id_type=MESH,
        )

    def left_copy(source, c, target):
        return pltpu.make_async_remote_copy(
            src_ref=source.at[c, target], dst_ref=in_l.at[c, target],
            send_sem=send_l.at[c, target], recv_sem=recv_l.at[c, target],
            device_id={"tp": before}, device_id_type=MESH,
        )

    @pl.when(spot == 0)
    def _():
        in_r[:, 0] = jnp.zeros_like(in_r[:, 0])

    @pl.when(spot == groups - 1)
    def _():
        in_l[:, groups - 1] = jnp.zeros_like(in_l[:, groups - 1])

    for c in range(chunks):
        product = mm(normed[...], weight[:, c * width : (c + 1) * width]).astype(bf16)
        part[c] = product.reshape(groups, rows, width)

        @pl.when(spot == 0)
        def _():
            for target in range(groups - 1, 0, -1):
                right_copy(part, c, target).start()

        @pl.when(spot == groups - 1)
        def _():
            for target in range(groups - 1):
                left_copy(part, c, target).start()

    for c in range(chunks):
        def relay(step, carry):
            far = groups - 1 - step

            @pl.when((spot > 0) & (far > spot))
            def _():
                right_copy(part, c, far).wait_recv()
                out_r[c, far] = (in_r[c, far].astype(f32) + part[c, far].astype(f32)).astype(bf16)
                right_copy(out_r, c, far).start()

            @pl.when((spot < groups - 1) & (step < spot))
            def _():
                left_copy(part, c, step).wait_recv()
                out_l[c, step] = (in_l[c, step].astype(f32) + part[c, step].astype(f32)).astype(bf16)
                left_copy(out_l, c, step).start()

            return carry

        lax.fori_loop(0, groups - 1, relay, 0)

    for c in range(chunks):
        @pl.when(spot > 0)
        def _():
            right_copy(part, c, spot).wait_recv()

        @pl.when(spot < groups - 1)
        def _():
            left_copy(part, c, spot).wait_recv()

        mixed = part[c, spot].astype(f32) + in_r[c, spot].astype(f32) + in_l[c, spot].astype(f32)
        out_ref[:, c * width : (c + 1) * width] = mixed.astype(bf16)

    for head in range(heads):
        @pl.when((me != head * apart) & (me < n - 1))
        def _():
            map_copy(head, me, head * apart).wait_send()

    for target in range(1, n):
        @pl.when(owner & (me != target))
        def _():
            state_copy(my_head, target).wait_send()

    for c in range(chunks):
        def drain(target, carry):
            @pl.when(target > spot)
            def _():
                right_copy(part, c, target).wait_send()

            @pl.when(target < spot)
            def _():
                left_copy(part, c, target).wait_send()

            return carry

        lax.fori_loop(0, groups, drain, 0)


def local(n, groups, queries, key_vectors, value_vectors, output_gate, write_rate, log_decay, norm_gain, out_weight):
    tokens = queries.shape[0]
    heads = value_vectors.shape[1] // DV
    features, model = out_weight.shape
    rows = tokens // groups
    chunks = 4
    width = model // chunks
    piece = pltpu.VMEM((chunks, groups, rows, width), bf16)
    dma = pltpu.SemaphoreType.DMA
    inputs = (
        queries, key_vectors, value_vectors, output_gate,
        write_rate.T, log_decay.T, norm_gain.reshape(1, DV), out_weight,
    )
    return pl.pallas_call(
        functools.partial(layer_kernel, n, groups),
        in_specs=[pl.BlockSpec(memory_space=pl.ANY)] * len(inputs),
        out_specs=pl.BlockSpec(memory_space=pltpu.VMEM),
        out_shape=jax.ShapeDtypeStruct((rows, model), bf16),
        scratch_shapes=[pltpu.VMEM(array.shape, array.dtype) for array in inputs] + [
            pltpu.VMEM((heads, DK, DK + DV), bf16),
            pltpu.VMEM((tokens, features), bf16),
            pltpu.VMEM((tokens, features), f32),
            pltpu.VMEM((tokens, features), f32),
            pltpu.VMEM((n, DK, DK + DV), bf16),
            pltpu.VMEM((n, DK, DV), bf16),
            pltpu.VMEM((heads, DK, DV), bf16),
            pltpu.VMEM((tokens, features), bf16),
            piece, piece, piece, piece, piece,
            dma((len(inputs),)), dma((heads,)), dma((n,)), dma((n,)), dma((heads,)),
            dma((chunks, groups)), dma((chunks, groups)), dma((chunks, groups)), dma((chunks, groups)),
        ],
        compiler_params=pltpu.CompilerParams(
            collective_id=0, has_side_effects=True, vmem_limit_bytes=56 * 2**20
        ),
    )(*inputs)


def solution(mesh):
    placed = (
        P("ctx", "tp"),
        P("ctx", "tp"),
        P("ctx", "tp"),
        P("ctx", "tp"),
        P("ctx", "tp"),
        P("ctx", "tp"),
        P(),
        P("tp", None),
    )
    body = functools.partial(local, mesh.shape["ctx"], mesh.shape["tp"])
    return jax.shard_map(
        body, mesh=mesh, in_specs=placed, out_specs=P(("ctx", "tp"), None), check_vma=False
    )
```

time: 91.8 us -> 61.6 us (0.67)
  the two profiles are of different devices: /device:TPU:4 before, /device:TPU:2 now
where the time goes in v2:
time: 61.6 us; the launch traced here: 61.4 us
  Pallas kernels  59.7 us (97%)
  local copies, waits for them, and re-layouts  1.67 us (3%)
    pallas_call x1, Pallas kernels, local(): pl.pallas_call(functools.partial(layer_kernel, n, groups), in_specs=[pl.B...  59.7 us
    unnamed x1, local copies, waits for them, and re-layouts  1.67 us

profile of v2, /device:TPU:2, one launch (start us, length us, event | category | flops | bytes accessed | tf_op | source)
XLA Modules:
  0.0 61.4 jit_solution(6049265169543167967)
XLA Ops:
  0.0 59.7 %shard_map.82 = bf16[64,2048]{1,0:T(8,128)(2,1)} custom-call(bf16[256,512]{1,0:T(8,128)(2,1)} %q_hbm.1, bf16[256,512]{1,0:T(8,128)(2,1)} %k_hbm.1, bf16[256,1024]{1,0:T(8,128)(2,1)} %v_hbm.1, bf16[256,1024]{1,0:T(8,128)(2,1)} %gate_hbm.1, f32[8,256]{1,0:T(8,128)} %bitcast.3, f32[8,256]{1,0:T(8,128)} %bitcast.4, f32[1,128]{1,0:T(1,128)} %bitcast.5, ...), custom_call_target="tpu_custom_call" | custom-call | tf_op jit(solution)/shard_map/pallas_call | solution.py:353
  59.7 1.7 %copy.10 = bf16[64,2048]{1,0:T(8,128)(2,1)} copy(bf16[64,2048]{1,0:T(8,128)(2,1)} %shard_map.82) | data formatting | bytes 524288

commit v3 on v2

--- a/solution.py
+++ b/solution.py
@@ -52,14 +52,11 @@
     return [r.astype(f32) + mm(r, residual) for r, residual in zip(rounded, residuals)]
 
 
-def summarize(groups, sharing, q_ref, k_ref, v_ref, rate_ref, decay_ref, map_ref, read_ref, own_ref):
+def prepare(key_heads, sharing, q_ref, k_ref, rate_ref, decay_ref, scores_ref):
     tokens = q_ref.shape[0]
-    half = tokens // 2
     row = lax.broadcasted_iota(jnp.int32, (tokens, tokens), 0)
     col = lax.broadcasted_iota(jnp.int32, (tokens, tokens), 1)
     eye, inclusive, strict = row == col, row >= col, row > col
-    key_row = lax.broadcasted_iota(jnp.int32, (DK, DK), 0)
-    key_col = lax.broadcasted_iota(jnp.int32, (DK, DK), 1)
 
     def to_row(column):
         return jnp.sum(jnp.where(eye, column, 0.0), axis=0, keepdims=True)
@@ -68,7 +65,7 @@
         return jnp.sum(jnp.where(eye, line, 0.0), axis=1, keepdims=True)
 
     parts = []
-    for group in groups:
+    for group in range(key_heads):
         key_place = slice(group * DK, (group + 1) * DK)
         queries, keys = q_ref[:, key_place], k_ref[:, key_place]
         queries_f, keys_f = queries.astype(f32), keys.astype(f32)
@@ -87,48 +84,55 @@
             erase_row = rate_row * jnp.exp(total_row) * key_scale_row
             ratios = jnp.where(inclusive, jnp.exp(jnp.where(inclusive, total - total_row, 0.0)), 0.0)
             ratios = ratios * key_scale_row
-            scores = (reads * ratios).astype(bf16)
+            scores_ref[head] = (reads * ratios).astype(bf16)
             lower = jnp.where(strict, rate * gram * ratios, 0.0)
-            read = jnp.exp(total) * query_scale * queries_f
-            parts.append((head, keys, key_scale, rate_row, erase_row, total, scores, lower, read))
-
+            read_scale = jnp.exp(total) * query_scale
+            closing = total[tokens - 1 :, :]
+            write_scale = jnp.exp(closing - total) * key_scale
+            parts.append((rate_row, erase_row, write_scale, jnp.exp(closing), read_scale, lower))
+    return parts
+
+
+def invert(parts):
+    half = parts[0][5].shape[0] // 2
     inverses = unit_lower_inverses(
-        [block for part in parts for block in (part[7][:half, :half], part[7][half:, half:])]
+        [block for part in parts for block in (part[5][:half, :half], part[5][half:, half:])]
     )
     firsts, seconds = inverses[0::2], inverses[1::2]
     inner = [
-        mm(part[7][half:, :half].astype(bf16), first.astype(bf16)).astype(bf16)
+        mm(part[5][half:, :half].astype(bf16), first.astype(bf16)).astype(bf16)
         for part, first in zip(parts, firsts)
     ]
     corners = [-mm(second.astype(bf16), i) for second, i in zip(seconds, inner)]
-
-    for part, first, second, corner in zip(parts, firsts, seconds, corners):
-        head, keys, key_scale, rate_row, erase_row, total, scores, _, read = part
-        place = slice(head * DV, (head + 1) * DV)
-
-        def solved(scale_row, right):
-            left_scale, right_scale = scale_row[:, :half], scale_row[:, half:]
-            top = mm((first * left_scale).astype(bf16), right[:half])
-            bottom = mm((corner * left_scale).astype(bf16), right[:half])
-            bottom += mm((second * right_scale).astype(bf16), right[half:])
-            return jnp.concatenate([top, bottom], axis=0)
-
-        both = jnp.concatenate([solved(erase_row, keys), solved(rate_row, v_ref[:, place])], axis=1)
-        closing = total[tokens - 1 :, :]
-        weight = jnp.exp(closing - total) * key_scale
-        summary = mm_cols(keys, (both * weight).astype(bf16))
-        moved = jnp.where(key_row == key_col, jnp.exp(closing), 0.0) - summary[:, :DK]
-        map_ref[head, :, :DK] = moved.astype(bf16)
-        map_ref[head, :, DK:] = summary[:, DK:].astype(bf16)
-        seen = mm(scores, both.astype(bf16))
-        read_ref[:, place] = (read - seen[:, :DK]).astype(bf16)
-        own_ref[:, place] = seen[:, DK:]
+    return list(zip(firsts, seconds, corners))
+
+
+def head_map(part, blocks, keys, values, map_ref, both_ref):
+    rate_row, erase_row, write_scale, fade = part[:4]
+    first, second, corner = blocks
+    half = first.shape[0]
+    key_row = lax.broadcasted_iota(jnp.int32, (DK, DK), 0)
+    key_col = lax.broadcasted_iota(jnp.int32, (DK, DK), 1)
+
+    def solved(scale_row, right):
+        left_scale, right_scale = scale_row[:, :half], scale_row[:, half:]
+        top = mm((first * left_scale).astype(bf16), right[:half])
+        bottom = mm((corner * left_scale).astype(bf16), right[:half])
+        bottom += mm((second * right_scale).astype(bf16), right[half:])
+        return jnp.concatenate([top, bottom], axis=0)
+
+    both = jnp.concatenate([solved(erase_row, keys), solved(rate_row, values)], axis=1)
+    both_ref[...] = both.astype(bf16)
+    summary = mm_cols(keys, (both * write_scale).astype(bf16))
+    moved = jnp.where(key_row == key_col, fade, 0.0) - summary[:, :DK]
+    map_ref[:, :DK] = moved.astype(bf16)
+    map_ref[:, DK:] = summary[:, DK:].astype(bf16)
 
 
 def layer_kernel(
     n, groups, q_hbm, k_hbm, v_hbm, gate_hbm, rate_hbm, decay_hbm, gain_hbm, weight_hbm, out_ref,
     q_ref, k_ref, v_ref, gate_ref, rate_ref, decay_ref, gain_ref, weight,
-    map_ref, read_ref, own_ref, gating,
+    map_ref, read_ref, own_ref, gating, scores_ref, both_ref,
     arrived, leaving, state, normed, part, out_r, out_l, in_r, in_l,
     load_sem, map_send, map_recv, state_send, state_recv,
     send_r, recv_r, send_l, recv_l,
@@ -147,7 +151,7 @@
             (v_hbm, v_ref), (gain_hbm, gain_ref), (gate_hbm, gate_ref), (weight_hbm, weight),
         ))
     ]
-    for load in loads:
+    for load in loads[:4]:
         load.start()
 
     barrier = pltpu.get_barrier_semaphore()
@@ -176,21 +180,34 @@
 
     key_heads = k_ref.shape[1] // DK
     sharing = heads // key_heads
-    batch = min(2, key_heads)
-    for load in loads[:5]:
+    for load in loads[:4]:
         load.wait()
-
-    for start in range(0, key_heads, batch):
-        summarize(
-            range(start, start + batch), sharing,
-            q_ref, k_ref, v_ref, rate_ref, decay_ref, map_ref, read_ref, own_ref,
+    for load in loads[4:]:
+        load.start()
+    parts = prepare(key_heads, sharing, q_ref, k_ref, rate_ref, decay_ref, scores_ref)
+    blocks = invert(parts)
+    loads[4].wait()
+    for head in range(heads):
+        place = slice(head * DV, (head + 1) * DV)
+        group = head // sharing
+        keys = k_ref[:, group * DK : (group + 1) * DK]
+        head_map(
+            parts[head], blocks[head], keys, v_ref[:, place], map_ref.at[head], both_ref.at[head]
         )
-        if start == 0:
+        if head == 0:
             pl.semaphore_wait(barrier, n - 1 + peers)
-        for head in range(start * sharing, (start + batch) * sharing):
-            @pl.when((me != head * apart) & (me < n - 1))
-            def _():
-                map_copy(head, me, head * apart).start()
+
+        @pl.when((me != head * apart) & (me < n - 1))
+        def _():
+            map_copy(head, me, head * apart).start()
+
+    for head in range(heads):
+        place = slice(head * DV, (head + 1) * DV)
+        group = head // sharing
+        queries = q_ref[:, group * DK : (group + 1) * DK].astype(f32)
+        seen = mm(scores_ref[head], both_ref[head])
+        read_ref[:, place] = (parts[head][4] * queries - seen[:, :DK]).astype(bf16)
+        own_ref[:, place] = seen[:, DK:]
 
     for load in loads[5:]:
         load.wait()
@@ -266,19 +283,28 @@
     def _():
         in_l[:, groups - 1] = jnp.zeros_like(in_l[:, groups - 1])
 
+    to_right = [(c, target) for c in range(chunks) for target in range(groups - 1, 0, -1)]
+    to_left = [(c, target) for c in range(chunks) for target in range(groups - 1)]
+    window = 2
+
+    def feed(copy, order, c):
+        for i, unit in enumerate(order):
+            if unit[0] == c:
+                if i >= window:
+                    copy(part, *order[i - window]).wait_send()
+                copy(part, *unit).start()
+
     for c in range(chunks):
         product = mm(normed[...], weight[:, c * width : (c + 1) * width]).astype(bf16)
         part[c] = product.reshape(groups, rows, width)
 
         @pl.when(spot == 0)
         def _():
-            for target in range(groups - 1, 0, -1):
-                right_copy(part, c, target).start()
+            feed(right_copy, to_right, c)
 
         @pl.when(spot == groups - 1)
         def _():
-            for target in range(groups - 1):
-                left_copy(part, c, target).start()
+            feed(left_copy, to_left, c)
 
     for c in range(chunks):
         def relay(step, carry):
@@ -324,17 +350,27 @@
 
     for c in range(chunks):
         def drain(target, carry):
-            @pl.when(target > spot)
+            @pl.when((target > spot) & (spot > 0))
             def _():
                 right_copy(part, c, target).wait_send()
 
-            @pl.when(target < spot)
+            @pl.when((target < spot) & (spot < groups - 1))
             def _():
                 left_copy(part, c, target).wait_send()
 
             return carry
 
         lax.fori_loop(0, groups, drain, 0)
+
+    @pl.when(spot == 0)
+    def _():
+        for unit in to_right[-window:]:
+            right_copy(part, *unit).wait_send()
+
+    @pl.when(spot == groups - 1)
+    def _():
+        for unit in to_left[-window:]:
+            left_copy(part, *unit).wait_send()
 
 
 def local(n, groups, queries, key_vectors, value_vectors, output_gate, write_rate, log_decay, norm_gain, out_weight):
@@ -360,6 +396,8 @@
             pltpu.VMEM((tokens, features), bf16),
             pltpu.VMEM((tokens, features), f32),
             pltpu.VMEM((tokens, features), f32),
+            pltpu.VMEM((heads, tokens, tokens), bf16),
+            pltpu.VMEM((heads, tokens, DK + DV), bf16),
             pltpu.VMEM((n, DK, DK + DV), bf16),
             pltpu.VMEM((n, DK, DV), bf16),
             pltpu.VMEM((heads, DK, DV), bf16),
@@ -369,7 +407,7 @@
             dma((chunks, groups)), dma((chunks, groups)), dma((chunks, groups)), dma((chunks, groups)),
         ],
         compiler_params=pltpu.CompilerParams(
-            collective_id=0, has_side_effects=True, vmem_limit_bytes=56 * 2**20
+            collective_id=0, has_side_effects=True, vmem_limit_bytes=40 * 2**20
         ),
     )(*inputs)
 

time: 61.6 us -> 66.5 us (1.080)
  the two profiles are of different devices: /device:TPU:2 before, /device:TPU:4 now
where the time goes in v3:
time: 66.5 us; the launch traced here: 66.1 us
  Pallas kernels  57.2 us (86%)
  local copies, waits for them, and re-layouts  8.92 us (13%)
    pallas_call x1, Pallas kernels, local(): pl.pallas_call(functools.partial(layer_kernel, n, groups), in_specs=[pl.B...  57.2 us
    unnamed x17, local copies, waits for them, and re-layouts  8.92 us

profile of v3, /device:TPU:4, one launch (start us, length us, event | category | flops | bytes accessed | tf_op | source)
XLA Modules:
  0.0 66.1 jit_solution(4854771905581426525)
XLA Ops:
  0.0 0.0 copy-start
  0.0 2.2 %copy-done = bf16[1024,2048]{1,0:T(8,128)(2,1)S(1)} copy-done((bf16[1024,2048]{1,0:T(8,128)(2,1)S(1)}, bf16[1024,2048]{1,0:T(8,128)(2,1)}, u32[]{:S(2)}) %copy-start) | copy-done | bytes 4194328
  2.2 0.0 copy-start.1
  2.2 1.0 %copy-done.1 = bf16[256,1024]{1,0:T(8,128)(2,1)S(1)} copy-done((bf16[256,1024]{1,0:T(8,128)(2,1)S(1)}, bf16[256,1024]{1,0:T(8,128)(2,1)}, u32[]{:S(2)}) %copy-start.1) | copy-done | bytes 524312
  3.2 0.0 copy-start.2
  3.2 1.0 %copy-done.2 = bf16[256,1024]{1,0:T(8,128)(2,1)S(1)} copy-done((bf16[256,1024]{1,0:T(8,128)(2,1)S(1)}, bf16[256,1024]{1,0:T(8,128)(2,1)}, u32[]{:S(2)}) %copy-start.2) | copy-done | bytes 524312
  4.3 0.0 copy-start.3
  4.3 0.9 %copy-done.3 = bf16[256,512]{1,0:T(8,128)(2,1)S(1)} copy-done((bf16[256,512]{1,0:T(8,128)(2,1)S(1)}, bf16[256,512]{1,0:T(8,128)(2,1)}, u32[]{:S(2)}) %copy-start.3) | copy-done | bytes 262168
  5.2 0.0 copy-start.4
  5.2 0.9 %copy-done.4 = bf16[256,512]{1,0:T(8,128)(2,1)S(1)} copy-done((bf16[256,512]{1,0:T(8,128)(2,1)S(1)}, bf16[256,512]{1,0:T(8,128)(2,1)}, u32[]{:S(2)}) %copy-start.4) | copy-done | bytes 262168
  6.2 0.0 copy-start.5
  6.2 0.7 %copy-done.5 = f32[256,8]{0,1:T(8,128)S(1)} copy-done((f32[256,8]{0,1:T(8,128)S(1)}, f32[256,8]{0,1:T(8,128)}, u32[]{:S(2)}) %copy-start.5) | copy-done | bytes 8216
  6.9 0.0 copy-start.6
  6.9 0.7 %copy-done.6 = f32[256,8]{0,1:T(8,128)S(1)} copy-done((f32[256,8]{0,1:T(8,128)S(1)}, f32[256,8]{0,1:T(8,128)}, u32[]{:S(2)}) %copy-start.6) | copy-done | bytes 8216
  7.6 0.0 copy-start.7
  7.6 0.7 copy-done.7
  8.2 57.2 %shard_map.82 = bf16[64,2048]{1,0:T(8,128)(2,1)S(1)} custom-call(bf16[256,512]{1,0:T(8,128)(2,1)S(1)} %copy-done.3, bf16[256,512]{1,0:T(8,128)(2,1)S(1)} %copy-done.4, bf16[256,1024]{1,0:T(8,128)(2,1)S(1)} %copy-done.1, bf16[256,1024]{1,0:T(8,128)(2,1)S(1)} %copy-done.2, f32[8,256]{1,0:T(8,128)S(1)} %bitcast.3, f32[8,256]{1,0:T(8,128)S(1)} %bitcast.4, ...), custom_call_target="tpu_custom_call" | custom-call | tf_op jit(solution)/shard_map/pallas_call | solution.py:389
  65.4 0.7 %copy.10 = bf16[64,2048]{1,0:T(8,128)(2,1)} copy(bf16[64,2048]{1,0:T(8,128)(2,1)S(1)} %shard_map.82) | data formatting | bytes 524288
Async XLA Ops:
  0.0 2.2 %copy-start = (bf16[1024,2048]{1,0:T(8,128)(2,1)S(1)}, bf16[1024,2048]{1,0:T(8,128)(2,1)}, u32[]{:S(2)}) copy-start(bf16[1024,2048]{1,0:T(8,128)(2,1)} %weight_hbm.1) | copy-start | bytes 12582916
  2.2 1.0 %copy-start.1 = (bf16[256,1024]{1,0:T(8,128)(2,1)S(1)}, bf16[256,1024]{1,0:T(8,128)(2,1)}, u32[]{:S(2)}) copy-start(bf16[256,1024]{1,0:T(8,128)(2,1)} %v_hbm.1) | copy-start | bytes 1572868
  3.2 1.0 %copy-start.2 = (bf16[256,1024]{1,0:T(8,128)(2,1)S(1)}, bf16[256,1024]{1,0:T(8,128)(2,1)}, u32[]{:S(2)}) copy-start(bf16[256,1024]{1,0:T(8,128)(2,1)} %gate_hbm.1) | copy-start | bytes 1572868
  4.3 0.9 %copy-start.3 = (bf16[256,512]{1,0:T(8,128)(2,1)S(1)}, bf16[256,512]{1,0:T(8,128)(2,1)}, u32[]{:S(2)}) copy-start(bf16[256,512]{1,0:T(8,128)(2,1)} %q_hbm.1) | copy-start | bytes 786436
  5.2 0.9 %copy-start.4 = (bf16[256,512]{1,0:T(8,128)(2,1)S(1)}, bf16[256,512]{1,0:T(8,128)(2,1)}, u32[]{:S(2)}) copy-start(bf16[256,512]{1,0:T(8,128)(2,1)} %k_hbm.1) | copy-start | bytes 786436
  6.2 0.7 %copy-start.5 = (f32[256,8]{0,1:T(8,128)S(1)}, f32[256,8]{0,1:T(8,128)}, u32[]{:S(2)}) copy-start(f32[256,8]{0,1:T(8,128)} %param.12) | copy-start | bytes 24580
  6.9 0.7 %copy-start.6 = (f32[256,8]{0,1:T(8,128)S(1)}, f32[256,8]{0,1:T(8,128)}, u32[]{:S(2)}) copy-start(f32[256,8]{0,1:T(8,128)} %param.13) | copy-start | bytes 24580
  7.6 0.7 copy-start.7

commit v4 on v3

--- a/solution.py
+++ b/solution.py
@@ -52,57 +52,79 @@
     return [r.astype(f32) + mm(r, residual) for r, residual in zip(rounded, residuals)]
 
 
-def prepare(key_heads, sharing, q_ref, k_ref, rate_ref, decay_ref, scores_ref):
-    tokens = q_ref.shape[0]
+def square_sums(source, key_heads, sharing):
+    lane = lax.broadcasted_iota(jnp.int32, (DK, 128), 1)
+    sums = 0.0
+    for group in range(key_heads):
+        mine = (lane >= group * sharing) & (lane < (group + 1) * sharing)
+        chosen = jnp.where(mine, 1.0, 0.0).astype(bf16)
+        values = source[:, group * DK : (group + 1) * DK].astype(f32)
+        squares = values * values
+        high = squares.astype(bf16)
+        sums = sums + mm(high, chosen) + mm((squares - high.astype(f32)).astype(bf16), chosen)
+    return sums
+
+
+def prepare(key_heads, sharing, q_ref, k_ref, rate_ref, decay_ref, turn_ref, scores_ref):
+    tokens, heads = q_ref.shape[0], rate_ref.shape[0]
+    half = tokens // 2
     row = lax.broadcasted_iota(jnp.int32, (tokens, tokens), 0)
     col = lax.broadcasted_iota(jnp.int32, (tokens, tokens), 1)
-    eye, inclusive, strict = row == col, row >= col, row > col
-
-    def to_row(column):
-        return jnp.sum(jnp.where(eye, column, 0.0), axis=0, keepdims=True)
-
-    def to_col(line):
-        return jnp.sum(jnp.where(eye, line, 0.0), axis=1, keepdims=True)
-
+    upper = jnp.where(row <= col, 1.0, 0.0)
+    total_rows = jnp.dot(
+        decay_ref[...], upper, precision=lax.Precision.HIGHEST, preferred_element_type=f32
+    )
+    rate_rows = rate_ref[...]
+    turn_ref[...] = jnp.zeros_like(turn_ref)
+    turn_ref[0, :heads] = rate_rows
+    turn_ref[1, :heads] = total_rows
+    rate, total = turn_ref[0].T, turn_ref[1].T
+    key_scale = lax.rsqrt(square_sums(k_ref, key_heads, sharing) + 1e-06)
+    query_scale = lax.rsqrt(square_sums(q_ref, key_heads, sharing) + 1e-06)
+    key_rows = key_scale.T[:heads]
+    erase_rows = rate_rows * jnp.exp(total_rows) * key_rows
+    closing = total[tokens - 1 :, :]
+    fade = jnp.exp(closing)
+    write_scale = jnp.exp(closing - total) * key_scale
+    strength = rate * key_scale
+
+    half_row = lax.broadcasted_iota(jnp.int32, (half, half), 0)
+    half_col = lax.broadcasted_iota(jnp.int32, (half, half), 1)
+    inclusive, strict = half_row >= half_col, half_row > half_col
     parts = []
     for group in range(key_heads):
         key_place = slice(group * DK, (group + 1) * DK)
         queries, keys = q_ref[:, key_place], k_ref[:, key_place]
-        queries_f, keys_f = queries.astype(f32), keys.astype(f32)
-        query_scale = lax.rsqrt(jnp.sum(queries_f * queries_f, axis=1, keepdims=True) + 1e-06)
-        key_scale = lax.rsqrt(jnp.sum(keys_f * keys_f, axis=1, keepdims=True) + 1e-06)
-        key_scale_row = to_row(key_scale)
-        gram = mm_rows(keys, keys) * key_scale
-        reads = mm_rows(queries, keys) * query_scale
-        for member in range(sharing):
-            head = group * sharing + member
-            rate_row = rate_ref[head : head + 1, :]
-            decay_row = decay_ref[head : head + 1, :]
-            rate, decay = to_col(rate_row), to_col(decay_row)
-            total_row = jnp.sum(jnp.where(row <= col, decay, 0.0), axis=0, keepdims=True)
-            total = to_col(total_row)
-            erase_row = rate_row * jnp.exp(total_row) * key_scale_row
-            ratios = jnp.where(inclusive, jnp.exp(jnp.where(inclusive, total - total_row, 0.0)), 0.0)
-            ratios = ratios * key_scale_row
-            scores_ref[head] = (reads * ratios).astype(bf16)
-            lower = jnp.where(strict, rate * gram * ratios, 0.0)
-            read_scale = jnp.exp(total) * query_scale
-            closing = total[tokens - 1 :, :]
-            write_scale = jnp.exp(closing - total) * key_scale
-            parts.append((rate_row, erase_row, write_scale, jnp.exp(closing), read_scale, lower))
+        gram = mm_rows(keys, keys)
+        reads = mm_rows(queries, keys)
+        for head in range(group * sharing, (group + 1) * sharing):
+            here = slice(head, head + 1)
+            total_row, key_row = total_rows[here], key_rows[here]
+
+            def spread(rows, cols):
+                return jnp.exp(total[rows, here] - total_row[:, cols])
+
+            top, low = slice(0, half), slice(half, tokens)
+            ratio_a = jnp.where(inclusive, spread(top, top), 0.0) * key_row[:, top]
+            ratio_b = jnp.where(inclusive, spread(low, low), 0.0) * key_row[:, low]
+            ratio_c = spread(low, top) * key_row[:, top]
+            scores_ref[head, :half, :half] = (reads[top, top] * ratio_a).astype(bf16)
+            scores_ref[head, half:, :half] = (reads[low, top] * ratio_c).astype(bf16)
+            scores_ref[head, half:, half:] = (reads[low, low] * ratio_b).astype(bf16)
+            lower_a = jnp.where(strict, gram[top, top] * ratio_a * strength[top, here], 0.0)
+            lower_b = jnp.where(strict, gram[low, low] * ratio_b * strength[low, here], 0.0)
+            lower_c = (gram[low, top] * ratio_c * strength[low, here]).astype(bf16)
+            parts.append((
+                rate_rows[here], erase_rows[here], write_scale[:, here], fade[:, here],
+                jnp.exp(total[:, here]), query_scale[:, here], lower_a, lower_b, lower_c,
+            ))
     return parts
 
 
 def invert(parts):
-    half = parts[0][5].shape[0] // 2
-    inverses = unit_lower_inverses(
-        [block for part in parts for block in (part[5][:half, :half], part[5][half:, half:])]
-    )
+    inverses = unit_lower_inverses([block for part in parts for block in part[6:8]])
     firsts, seconds = inverses[0::2], inverses[1::2]
-    inner = [
-        mm(part[5][half:, :half].astype(bf16), first.astype(bf16)).astype(bf16)
-        for part, first in zip(parts, firsts)
-    ]
+    inner = [mm(part[8], first.astype(bf16)).astype(bf16) for part, first in zip(parts, firsts)]
     corners = [-mm(second.astype(bf16), i) for second, i in zip(seconds, inner)]
     return list(zip(firsts, seconds, corners))
 
@@ -132,7 +154,7 @@
 def layer_kernel(
     n, groups, q_hbm, k_hbm, v_hbm, gate_hbm, rate_hbm, decay_hbm, gain_hbm, weight_hbm, out_ref,
     q_ref, k_ref, v_ref, gate_ref, rate_ref, decay_ref, gain_ref, weight,
-    map_ref, read_ref, own_ref, gating, scores_ref, both_ref,
+    map_ref, read_ref, own_ref, gating, turn_ref, scores_ref, both_ref,
     arrived, leaving, state, normed, part, out_r, out_l, in_r, in_l,
     load_sem, map_send, map_recv, state_send, state_recv,
     send_r, recv_r, send_l, recv_l,
@@ -184,7 +206,7 @@
         load.wait()
     for load in loads[4:]:
         load.start()
-    parts = prepare(key_heads, sharing, q_ref, k_ref, rate_ref, decay_ref, scores_ref)
+    parts = prepare(key_heads, sharing, q_ref, k_ref, rate_ref, decay_ref, turn_ref, scores_ref)
     blocks = invert(parts)
     loads[4].wait()
     for head in range(heads):
@@ -201,13 +223,17 @@
         def _():
             map_copy(head, me, head * apart).start()
 
+    half = q_ref.shape[0] // 2
     for head in range(heads):
         place = slice(head * DV, (head + 1) * DV)
         group = head // sharing
         queries = q_ref[:, group * DK : (group + 1) * DK].astype(f32)
-        seen = mm(scores_ref[head], both_ref[head])
-        read_ref[:, place] = (parts[head][4] * queries - seen[:, :DK]).astype(bf16)
-        own_ref[:, place] = seen[:, DK:]
+        decayed, query_scale = parts[head][4:6]
+        top = mm(scores_ref[head, :half, :half], both_ref[head, :half])
+        low = mm(scores_ref[head, half:], both_ref[head])
+        seen = jnp.concatenate([top, low], axis=0)
+        read_ref[:, place] = ((decayed * queries - seen[:, :DK]) * query_scale).astype(bf16)
+        own_ref[:, place] = seen[:, DK:] * query_scale
 
     for load in loads[5:]:
         load.wait()
@@ -231,34 +257,38 @@
     @pl.when(owner)
     def _():
         arrived[pl.ds(me, 1)] = map_ref[pl.ds(my_head, 1)]
-        current = jnp.zeros((DK, DV), f32)
         for step in range(n - 1):
             @pl.when(me != step)
             def _():
                 map_copy(0, step, step).wait_recv()
 
-            high = current.astype(bf16)
-            low = (current - high.astype(f32)).astype(bf16)
-            turned = mm(arrived[step, :, :DK], jnp.concatenate([high, low], axis=1))
-            current = turned[:, :DV] + turned[:, DV:] + arrived[step, :, DK:].astype(f32)
+        current = arrived[0, :, DK:].astype(f32)
+        for step in range(n - 1):
+            if step > 0:
+                high = current.astype(bf16)
+                low = (current - high.astype(f32)).astype(bf16)
+                turned = mm(arrived[step, :, :DK], jnp.concatenate([high, low], axis=1))
+                current = turned[:, :DV] + turned[:, DV:] + arrived[step, :, DK:].astype(f32)
+            leaving[step + 1] = current.astype(bf16)
 
             @pl.when(me != step + 1)
             def _():
-                leaving[step + 1] = current.astype(bf16)
                 state_copy(my_head, step + 1).start()
 
-            @pl.when(me == step + 1)
-            def _():
-                state[pl.ds(my_head, 1)] = current.astype(bf16)[None]
+        @pl.when(me > 0)
+        def _():
+            state[pl.ds(my_head, 1)] = leaving[pl.ds(me, 1)]
 
     for head in range(heads):
         @pl.when((me > 0) & (me != head * apart))
         def _():
             state_copy(head, 0).wait_recv()
 
+    ones = jnp.ones((DV, DV), bf16)
+    for head in range(heads):
         place = slice(head * DV, (head + 1) * DV)
         core = mm(read_ref[:, place], state[head]) + own_ref[:, place]
-        square_mean = jnp.mean(core * core, axis=1, keepdims=True)
+        square_mean = mm((core * core).astype(bf16), ones) * (1.0 / DV)
         normed[:, place] = (core * lax.rsqrt(square_mean + 1e-06) * gating[:, place]).astype(bf16)
 
     def right_copy(source, c, target):
@@ -396,6 +426,7 @@
             pltpu.VMEM((tokens, features), bf16),
             pltpu.VMEM((tokens, features), f32),
             pltpu.VMEM((tokens, features), f32),
+            pltpu.VMEM((2, 128, tokens), f32),
             pltpu.VMEM((heads, tokens, tokens), bf16),
             pltpu.VMEM((heads, tokens, DK + DV), bf16),
             pltpu.VMEM((n, DK, DK + DV), bf16),
@@ -407,7 +438,7 @@
             dma((chunks, groups)), dma((chunks, groups)), dma((chunks, groups)), dma((chunks, groups)),
         ],
         compiler_params=pltpu.CompilerParams(
-            collective_id=0, has_side_effects=True, vmem_limit_bytes=40 * 2**20
+            collective_id=0, has_side_effects=True, vmem_limit_bytes=56 * 2**20
         ),
     )(*inputs)
 

time: 66.5 us -> 58.9 us (0.89)
  local copies, waits for them, and re-layouts: 8.92 us -> 1.67 us
    unnamed x17 -> x1, local copies, waits for them, and re-layouts: 8.92 us -> 1.67 us
where the time goes in v4:
time: 58.9 us; the launch traced here: 58.7 us
  Pallas kernels  57 us (97%)
  local copies, waits for them, and re-layouts  1.67 us (3%)
    pallas_call x1, Pallas kernels, local(): pl.pallas_call(functools.partial(layer_kernel, n, groups), in_specs=[pl.B...  57 us
    unnamed x1, local copies, waits for them, and re-layouts  1.67 us

profile of v4, /device:TPU:4, one launch (start us, length us, event | category | flops | bytes accessed | tf_op | source)
XLA Modules:
  0.0 58.7 jit_solution(9246720749390519863)
XLA Ops:
  0.0 57.0 %shard_map.82 = bf16[64,2048]{1,0:T(8,128)(2,1)} custom-call(bf16[256,512]{1,0:T(8,128)(2,1)} %q_hbm.1, bf16[256,512]{1,0:T(8,128)(2,1)} %k_hbm.1, bf16[256,1024]{1,0:T(8,128)(2,1)} %v_hbm.1, bf16[256,1024]{1,0:T(8,128)(2,1)} %gate_hbm.1, f32[8,256]{1,0:T(8,128)} %bitcast.3, f32[8,256]{1,0:T(8,128)} %bitcast.4, f32[1,128]{1,0:T(1,128)} %bitcast.5, ...), custom_call_target="tpu_custom_call" | custom-call | tf_op jit(solution)/shard_map/pallas_call | solution.py:419
  57.0 1.7 %copy.10 = bf16[64,2048]{1,0:T(8,128)(2,1)} copy(bf16[64,2048]{1,0:T(8,128)(2,1)} %shard_map.82) | data formatting | bytes 524288

commit v5 on v4

--- a/solution.py
+++ b/solution.py
@@ -152,17 +152,15 @@
 
 
 def layer_kernel(
-    n, groups, q_hbm, k_hbm, v_hbm, gate_hbm, rate_hbm, decay_hbm, gain_hbm, weight_hbm, out_ref,
-    q_ref, k_ref, v_ref, gate_ref, rate_ref, decay_ref, gain_ref, weight,
+    n, q_hbm, k_hbm, v_hbm, gate_hbm, rate_hbm, decay_hbm, gain_hbm, normed,
+    q_ref, k_ref, v_ref, gate_ref, rate_ref, decay_ref, gain_ref,
     map_ref, read_ref, own_ref, gating, turn_ref, scores_ref, both_ref,
-    arrived, leaving, state, normed, part, out_r, out_l, in_r, in_l,
+    arrived, leaving, state,
     load_sem, map_send, map_recv, state_send, state_recv,
-    send_r, recv_r, send_l, recv_l,
 ):
     heads = map_ref.shape[0]
     apart = n // heads
-    chunks, _, rows, width = part.shape
-    me, spot = lax.axis_index("ctx"), lax.axis_index("tp")
+    me = lax.axis_index("ctx")
     my_head = me // apart
     owner = lax.rem(me, apart) == 0
 
@@ -170,7 +168,7 @@
         pltpu.make_async_copy(source, target, load_sem.at[i])
         for i, (source, target) in enumerate((
             (k_hbm, k_ref), (q_hbm, q_ref), (rate_hbm, rate_ref), (decay_hbm, decay_ref),
-            (v_hbm, v_ref), (gain_hbm, gain_ref), (gate_hbm, gate_ref), (weight_hbm, weight),
+            (v_hbm, v_ref), (gain_hbm, gain_ref), (gate_hbm, gate_ref),
         ))
     ]
     for load in loads[:4]:
@@ -182,17 +180,6 @@
         def _():
             pl.semaphore_signal(barrier, inc=1, device_id={"ctx": other}, device_id_type=MESH)
 
-    after, before = lax.rem(spot + 1, groups), lax.rem(spot + groups - 1, groups)
-
-    @pl.when(spot > 0)
-    def _():
-        pl.semaphore_signal(barrier, inc=1, device_id={"tp": before}, device_id_type=MESH)
-
-    @pl.when(spot < groups - 1)
-    def _():
-        pl.semaphore_signal(barrier, inc=1, device_id={"tp": after}, device_id_type=MESH)
-
-    peers = (spot > 0).astype(jnp.int32) + (spot < groups - 1).astype(jnp.int32)
     def map_copy(head, slot, target):
         return pltpu.make_async_remote_copy(
             src_ref=map_ref.at[head], dst_ref=arrived.at[slot],
@@ -217,7 +204,7 @@
             parts[head], blocks[head], keys, v_ref[:, place], map_ref.at[head], both_ref.at[head]
         )
         if head == 0:
-            pl.semaphore_wait(barrier, n - 1 + peers)
+            pl.semaphore_wait(barrier, n - 1)
 
         @pl.when((me != head * apart) & (me < n - 1))
         def _():
@@ -291,6 +278,36 @@
         square_mean = mm((core * core).astype(bf16), ones) * (1.0 / DV)
         normed[:, place] = (core * lax.rsqrt(square_mean + 1e-06) * gating[:, place]).astype(bf16)
 
+    for head in range(heads):
+        @pl.when((me != head * apart) & (me < n - 1))
+        def _():
+            map_copy(head, me, head * apart).wait_send()
+
+    for target in range(1, n):
+        @pl.when(owner & (me != target))
+        def _():
+            state_copy(my_head, target).wait_send()
+
+
+def sum_kernel(
+    groups, normed, weight, out_ref, part, out_r, out_l, in_r, in_l, send_r, recv_r, send_l, recv_l
+):
+    chunks, _, rows, width = part.shape
+    spot = lax.axis_index("tp")
+    after, before = lax.rem(spot + 1, groups), lax.rem(spot + groups - 1, groups)
+    barrier = pltpu.get_barrier_semaphore()
+
+    @pl.when(spot > 0)
+    def _():
+        pl.semaphore_signal(barrier, inc=1, device_id={"tp": before}, device_id_type=MESH)
+
+    @pl.when(spot < groups - 1)
+    def _():
+        pl.semaphore_signal(barrier, inc=1, device_id={"tp": after}, device_id_type=MESH)
+
+    peers = (spot > 0).astype(jnp.int32) + (spot < groups - 1).astype(jnp.int32)
+    pl.semaphore_wait(barrier, peers)
+
     def right_copy(source, c, target):
         return pltpu.make_async_remote_copy(
             src_ref=source.at[c, target], dst_ref=in_r.at[c, target],
@@ -367,16 +384,6 @@
 
         mixed = part[c, spot].astype(f32) + in_r[c, spot].astype(f32) + in_l[c, spot].astype(f32)
         out_ref[:, c * width : (c + 1) * width] = mixed.astype(bf16)
-
-    for head in range(heads):
-        @pl.when((me != head * apart) & (me < n - 1))
-        def _():
-            map_copy(head, me, head * apart).wait_send()
-
-    for target in range(1, n):
-        @pl.when(owner & (me != target))
-        def _():
-            state_copy(my_head, target).wait_send()
 
     for c in range(chunks):
         def drain(target, carry):
@@ -414,13 +421,13 @@
     dma = pltpu.SemaphoreType.DMA
     inputs = (
         queries, key_vectors, value_vectors, output_gate,
-        write_rate.T, log_decay.T, norm_gain.reshape(1, DV), out_weight,
+        write_rate.T, log_decay.T, norm_gain.reshape(1, DV),
     )
-    return pl.pallas_call(
-        functools.partial(layer_kernel, n, groups),
+    normed = pl.pallas_call(
+        functools.partial(layer_kernel, n),
         in_specs=[pl.BlockSpec(memory_space=pl.ANY)] * len(inputs),
         out_specs=pl.BlockSpec(memory_space=pltpu.VMEM),
-        out_shape=jax.ShapeDtypeStruct((rows, model), bf16),
+        out_shape=jax.ShapeDtypeStruct((tokens, features), bf16),
         scratch_shapes=[pltpu.VMEM(array.shape, array.dtype) for array in inputs] + [
             pltpu.VMEM((heads, DK, DK + DV), bf16),
             pltpu.VMEM((tokens, features), bf16),
@@ -432,15 +439,26 @@
             pltpu.VMEM((n, DK, DK + DV), bf16),
             pltpu.VMEM((n, DK, DV), bf16),
             pltpu.VMEM((heads, DK, DV), bf16),
-            pltpu.VMEM((tokens, features), bf16),
-            piece, piece, piece, piece, piece,
             dma((len(inputs),)), dma((heads,)), dma((n,)), dma((n,)), dma((heads,)),
-            dma((chunks, groups)), dma((chunks, groups)), dma((chunks, groups)), dma((chunks, groups)),
         ],
         compiler_params=pltpu.CompilerParams(
             collective_id=0, has_side_effects=True, vmem_limit_bytes=56 * 2**20
         ),
     )(*inputs)
+    vmem = pl.BlockSpec(memory_space=pltpu.VMEM)
+    return pl.pallas_call(
+        functools.partial(sum_kernel, groups),
+        in_specs=[vmem, vmem],
+        out_specs=vmem,
+        out_shape=jax.ShapeDtypeStruct((rows, model), bf16),
+        scratch_shapes=[
+            piece, piece, piece, piece, piece,
+            dma((chunks, groups)), dma((chunks, groups)), dma((chunks, groups)), dma((chunks, groups)),
+        ],
+        compiler_params=pltpu.CompilerParams(
+            collective_id=1, has_side_effects=True, vmem_limit_bytes=32 * 2**20
+        ),
+    )(normed, out_weight)
 
 
 def solution(mesh):

time: 58.9 us -> 62.9 us (1.068)
  local copies, waits for them, and re-layouts: 1.67 us -> 3.93 us
  Pallas kernels: 57 us -> 58.8 us
    unnamed x1 -> x5, local copies, waits for them, and re-layouts: 1.67 us -> 3.93 us
    pallas_call x1 -> x2, Pallas kernels: 57 us -> 58.8 us  [the longest x1 39.2 us: local(): pl.pallas_call(functools.partial(sum_kernel, groups), in_specs=[vmem, vme...]
where the time goes in v5:
time: 62.9 us; the launch traced here: 62.7 us
  Pallas kernels  58.8 us (93%)
  local copies, waits for them, and re-layouts  3.93 us (6%)
    pallas_call x1, Pallas kernels, local(): pl.pallas_call(functools.partial(sum_kernel, groups), in_specs=[vmem, vme...  39.2 us
    pallas_call x1, Pallas kernels, local(): pl.pallas_call(functools.partial(layer_kernel, n), in_specs=[pl.BlockSpec...  19.6 us
    unnamed x5, local copies, waits for them, and re-layouts  3.93 us

profile of v5, /device:TPU:4, one launch (start us, length us, event | category | flops | bytes accessed | tf_op | source)
XLA Modules:
  0.0 62.7 jit_solution(7101483098984174645)
XLA Ops:
  0.0 19.6 %shard_map.82.normed = bf16[256,1024]{1,0:T(8,128)(2,1)} custom-call(bf16[256,512]{1,0:T(8,128)(2,1)} %q_hbm.1, bf16[256,512]{1,0:T(8,128)(2,1)} %k_hbm.1, bf16[256,1024]{1,0:T(8,128)(2,1)} %v_hbm.1, bf16[256,1024]{1,0:T(8,128)(2,1)} %gate_hbm.1, f32[8,256]{1,0:T(8,128)} %bitcast.3, f32[8,256]{1,0:T(8,128)} %bitcast.4, f32[1,128]{1,0:T(1,128)} %bitcast.5), custom_call_target="tpu_custom_call" | custom-call | tf_op jit(solution)/shard_map/pallas_call | solution.py:426
  19.6 0.0 copy-start
  19.6 2.2 %copy-done = bf16[1024,2048]{1,0:T(8,128)(2,1)S(1)} copy-done((bf16[1024,2048]{1,0:T(8,128)(2,1)S(1)}, bf16[1024,2048]{1,0:T(8,128)(2,1)}, u32[]{:S(2)}) %copy-start) | copy-done | bytes 4194328
  21.8 0.0 copy-start.1
  21.8 1.0 %copy-done.1 = bf16[256,1024]{1,0:T(8,128)(2,1)S(1)} copy-done((bf16[256,1024]{1,0:T(8,128)(2,1)S(1)}, bf16[256,1024]{1,0:T(8,128)(2,1)}, u32[]{:S(2)}) %copy-start.1) | copy-done | bytes 524312
  22.8 39.2 %shard_map.83 = bf16[64,2048]{1,0:T(8,128)(2,1)S(1)} custom-call(bf16[256,1024]{1,0:T(8,128)(2,1)S(1)} %copy-done.1, bf16[1024,2048]{1,0:T(8,128)(2,1)S(1)} %copy-done), custom_call_target="tpu_custom_call" | custom-call | tf_op jit(solution)/shard_map/pallas_call | solution.py:449
  62.0 0.7 %copy.10 = bf16[64,2048]{1,0:T(8,128)(2,1)} copy(bf16[64,2048]{1,0:T(8,128)(2,1)S(1)} %shard_map.83) | data formatting | bytes 524288
Async XLA Ops:
  19.6 2.2 %copy-start = (bf16[1024,2048]{1,0:T(8,128)(2,1)S(1)}, bf16[1024,2048]{1,0:T(8,128)(2,1)}, u32[]{:S(2)}) copy-start(bf16[1024,2048]{1,0:T(8,128)(2,1)} %weight.1) | copy-start | bytes 12582916
  21.8 1.0 %copy-start.1 = (bf16[256,1024]{1,0:T(8,128)(2,1)S(1)}, bf16[256,1024]{1,0:T(8,128)(2,1)}, u32[]{:S(2)}) copy-start(bf16[256,1024]{1,0:T(8,128)(2,1)} %shard_map.82.normed) | copy-start | bytes 1572868

commit v6 on v4

--- a/solution.py
+++ b/solution.py
@@ -313,16 +313,13 @@
     def _():
         in_l[:, groups - 1] = jnp.zeros_like(in_l[:, groups - 1])
 
-    to_right = [(c, target) for c in range(chunks) for target in range(groups - 1, 0, -1)]
-    to_left = [(c, target) for c in range(chunks) for target in range(groups - 1)]
-    window = 2
-
-    def feed(copy, order, c):
-        for i, unit in enumerate(order):
-            if unit[0] == c:
-                if i >= window:
-                    copy(part, *order[i - window]).wait_send()
-                copy(part, *unit).start()
+    units = (groups - 1) * chunks
+
+    def right_unit(u):
+        return u % chunks, groups - 1 - u // chunks
+
+    def left_unit(u):
+        return u % chunks, u // chunks
 
     for c in range(chunks):
         product = mm(normed[...], weight[:, c * width : (c + 1) * width]).astype(bf16)
@@ -330,31 +327,48 @@
 
         @pl.when(spot == 0)
         def _():
-            feed(right_copy, to_right, c)
+            right_copy(part, *right_unit(c)).start()
 
         @pl.when(spot == groups - 1)
         def _():
-            feed(left_copy, to_left, c)
-
-    for c in range(chunks):
-        def relay(step, carry):
-            far = groups - 1 - step
-
-            @pl.when((spot > 0) & (far > spot))
-            def _():
-                right_copy(part, c, far).wait_recv()
-                out_r[c, far] = (in_r[c, far].astype(f32) + part[c, far].astype(f32)).astype(bf16)
-                right_copy(out_r, c, far).start()
-
-            @pl.when((spot < groups - 1) & (step < spot))
-            def _():
-                left_copy(part, c, step).wait_recv()
-                out_l[c, step] = (in_l[c, step].astype(f32) + part[c, step].astype(f32)).astype(bf16)
-                left_copy(out_l, c, step).start()
-
-            return carry
-
-        lax.fori_loop(0, groups - 1, relay, 0)
+            left_copy(part, *left_unit(c)).start()
+
+    @pl.when(spot == 0)
+    def _():
+        for u in range(chunks, units):
+            right_copy(part, *right_unit(u - chunks)).wait_send()
+            right_copy(part, *right_unit(u)).start()
+
+    @pl.when(spot == groups - 1)
+    def _():
+        for u in range(chunks, units):
+            left_copy(part, *left_unit(u - chunks)).wait_send()
+            left_copy(part, *left_unit(u)).start()
+
+    lag = 2
+
+    def relay(time, carry):
+        u = time - lag * (spot - 1)
+        c, target = u % chunks, groups - 1 - u // chunks
+
+        @pl.when((spot > 0) & (u >= 0) & (target > spot))
+        def _():
+            right_copy(part, c, target).wait_recv()
+            out_r[c, target] = (in_r[c, target].astype(f32) + part[c, target].astype(f32)).astype(bf16)
+            right_copy(out_r, c, target).start()
+
+        v = time - lag * (groups - 2 - spot)
+        d, goal = v % chunks, v // chunks
+
+        @pl.when((spot < groups - 1) & (v >= 0) & (goal < spot))
+        def _():
+            left_copy(part, d, goal).wait_recv()
+            out_l[d, goal] = (in_l[d, goal].astype(f32) + part[d, goal].astype(f32)).astype(bf16)
+            left_copy(out_l, d, goal).start()
+
+        return carry
+
+    lax.fori_loop(0, units + lag * (groups - 2), relay, 0)
 
     for c in range(chunks):
         @pl.when(spot > 0)
@@ -394,13 +408,13 @@
 
     @pl.when(spot == 0)
     def _():
-        for unit in to_right[-window:]:
-            right_copy(part, *unit).wait_send()
+        for u in range(units - chunks, units):
+            right_copy(part, *right_unit(u)).wait_send()
 
     @pl.when(spot == groups - 1)
     def _():
-        for unit in to_left[-window:]:
-            left_copy(part, *unit).wait_send()
+        for u in range(units - chunks, units):
+            left_copy(part, *left_unit(u)).wait_send()
 
 
 def local(n, groups, queries, key_vectors, value_vectors, output_gate, write_rate, log_decay, norm_gain, out_weight):

time: 58.9 us -> 42.4 us (0.72)
  the two profiles are of different devices: /device:TPU:4 before, /device:TPU:19 now
where the time goes in v6:
time: 42.4 us; the launch traced here: 42.2 us
  Pallas kernels  40.5 us (96%)
  local copies, waits for them, and re-layouts  1.67 us (4%)
    pallas_call x1, Pallas kernels, local(): pl.pallas_call(functools.partial(layer_kernel, n, groups), in_specs=[pl.B...  40.5 us
    unnamed x1, local copies, waits for them, and re-layouts  1.67 us

profile of v6, /device:TPU:19, one launch (start us, length us, event | category | flops | bytes accessed | tf_op | source)
XLA Modules:
  0.0 42.2 jit_solution(13601331897323120009)
XLA Ops:
  0.0 40.5 %shard_map.82 = bf16[64,2048]{1,0:T(8,128)(2,1)} custom-call(bf16[256,512]{1,0:T(8,128)(2,1)} %q_hbm.1, bf16[256,512]{1,0:T(8,128)(2,1)} %k_hbm.1, bf16[256,1024]{1,0:T(8,128)(2,1)} %v_hbm.1, bf16[256,1024]{1,0:T(8,128)(2,1)} %gate_hbm.1, f32[8,256]{1,0:T(8,128)} %bitcast.3, f32[8,256]{1,0:T(8,128)} %bitcast.4, f32[1,128]{1,0:T(1,128)} %bitcast.5, ...), custom_call_target="tpu_custom_call" | custom-call | tf_op jit(solution)/shard_map/pallas_call | solution.py:433
  40.5 1.7 %copy.10 = bf16[64,2048]{1,0:T(8,128)(2,1)} copy(bf16[64,2048]{1,0:T(8,128)(2,1)} %shard_map.82) | data formatting | bytes 524288

commit v7 on v6

--- a/solution.py
+++ b/solution.py
@@ -15,14 +15,6 @@
 
 def mm(left, right):
     return jnp.dot(left, right, preferred_element_type=f32)
-
-
-def mm_rows(left, right):
-    return lax.dot_general(left, right, (((1,), (1,)), ((), ())), preferred_element_type=f32)
-
-
-def mm_cols(left, right):
-    return lax.dot_general(left, right, (((0,), (0,)), ((), ())), preferred_element_type=f32)
 
 
 def unit_lower_inverses(lowers):
@@ -65,7 +57,7 @@
     return sums
 
 
-def prepare(key_heads, sharing, q_ref, k_ref, rate_ref, decay_ref, turn_ref, scores_ref):
+def prepare(key_heads, sharing, q_ref, k_ref, rate_ref, decay_ref, turn_ref, turned_ref, scores_ref):
     tokens, heads = q_ref.shape[0], rate_ref.shape[0]
     half = tokens // 2
     row = lax.broadcasted_iota(jnp.int32, (tokens, tokens), 0)
@@ -95,8 +87,10 @@
     for group in range(key_heads):
         key_place = slice(group * DK, (group + 1) * DK)
         queries, keys = q_ref[:, key_place], k_ref[:, key_place]
-        gram = mm_rows(keys, keys)
-        reads = mm_rows(queries, keys)
+        turned_keys = keys.T
+        turned_ref[group] = turned_keys
+        gram = mm(keys, turned_keys)
+        reads = mm(queries, turned_keys)
         for head in range(group * sharing, (group + 1) * sharing):
             here = slice(head, head + 1)
             total_row, key_row = total_rows[here], key_rows[here]
@@ -129,7 +123,7 @@
     return list(zip(firsts, seconds, corners))
 
 
-def head_map(part, blocks, keys, values, map_ref, both_ref):
+def head_map(part, blocks, keys, turned_keys, values, map_ref, both_ref):
     rate_row, erase_row, write_scale, fade = part[:4]
     first, second, corner = blocks
     half = first.shape[0]
@@ -145,7 +139,7 @@
 
     both = jnp.concatenate([solved(erase_row, keys), solved(rate_row, values)], axis=1)
     both_ref[...] = both.astype(bf16)
-    summary = mm_cols(keys, (both * write_scale).astype(bf16))
+    summary = mm(turned_keys, (both * write_scale).astype(bf16))
     moved = jnp.where(key_row == key_col, fade, 0.0) - summary[:, :DK]
     map_ref[:, :DK] = moved.astype(bf16)
     map_ref[:, DK:] = summary[:, DK:].astype(bf16)
@@ -154,7 +148,7 @@
 def layer_kernel(
     n, groups, q_hbm, k_hbm, v_hbm, gate_hbm, rate_hbm, decay_hbm, gain_hbm, weight_hbm, out_ref,
     q_ref, k_ref, v_ref, gate_ref, rate_ref, decay_ref, gain_ref, weight,
-    map_ref, read_ref, own_ref, gating, turn_ref, scores_ref, both_ref,
+    map_ref, read_ref, own_ref, gating, turn_ref, turned_ref, scores_ref, both_ref,
     arrived, leaving, state, normed, part, out_r, out_l, in_r, in_l,
     load_sem, map_send, map_recv, state_send, state_recv,
     send_r, recv_r, send_l, recv_l,
@@ -206,22 +200,25 @@
         load.wait()
     for load in loads[4:]:
         load.start()
-    parts = prepare(key_heads, sharing, q_ref, k_ref, rate_ref, decay_ref, turn_ref, scores_ref)
+    parts = prepare(key_heads, sharing, q_ref, k_ref, rate_ref, decay_ref, turn_ref, turned_ref, scores_ref)
     blocks = invert(parts)
     loads[4].wait()
-    for head in range(heads):
-        place = slice(head * DV, (head + 1) * DV)
-        group = head // sharing
-        keys = k_ref[:, group * DK : (group + 1) * DK]
-        head_map(
-            parts[head], blocks[head], keys, v_ref[:, place], map_ref.at[head], both_ref.at[head]
-        )
-        if head == 0:
+    together = min(4, heads)
+    for start in range(0, heads, together):
+        for head in range(start, start + together):
+            place = slice(head * DV, (head + 1) * DV)
+            group = head // sharing
+            keys = k_ref[:, group * DK : (group + 1) * DK]
+            head_map(
+                parts[head], blocks[head], keys, turned_ref[group], v_ref[:, place],
+                map_ref.at[head], both_ref.at[head],
+            )
+        if start == 0:
             pl.semaphore_wait(barrier, n - 1 + peers)
-
-        @pl.when((me != head * apart) & (me < n - 1))
-        def _():
-            map_copy(head, me, head * apart).start()
+        for head in range(start, start + together):
+            @pl.when((me != head * apart) & (me < n - 1))
+            def _():
+                map_copy(head, me, head * apart).start()
 
     half = q_ref.shape[0] // 2
     for head in range(heads):
@@ -441,6 +438,7 @@
             pltpu.VMEM((tokens, features), f32),
             pltpu.VMEM((tokens, features), f32),
             pltpu.VMEM((2, 128, tokens), f32),
+            pltpu.VMEM((queries.shape[1] // DK, DK, tokens), bf16),
             pltpu.VMEM((heads, tokens, tokens), bf16),
             pltpu.VMEM((heads, tokens, DK + DV), bf16),
             pltpu.VMEM((n, DK, DK + DV), bf16),

time: 42.4 us -> 42.8 us (level)
  Pallas kernels: 40.5 us -> 41 us
    pallas_call x1, Pallas kernels: 40.5 us -> 41 us  [local(): pl.pallas_call(functools.partial(layer_kernel, n, groups), in_specs=[pl.B...]
where the time goes in v7:
time: 42.8 us; the launch traced here: 42.7 us
  Pallas kernels  41 us (96%)
  local copies, waits for them, and re-layouts  1.67 us (4%)
    pallas_call x1, Pallas kernels, local(): pl.pallas_call(functools.partial(layer_kernel, n, groups), in_specs=[pl.B...  41 us
    unnamed x1, local copies, waits for them, and re-layouts  1.67 us

profile of v7, /device:TPU:19, one launch (start us, length us, event | category | flops | bytes accessed | tf_op | source)
XLA Modules:
  0.0 42.7 jit_solution(5345334707026701885)
XLA Ops:
  0.0 41.0 %shard_map.82 = bf16[64,2048]{1,0:T(8,128)(2,1)} custom-call(bf16[256,512]{1,0:T(8,128)(2,1)} %q_hbm.1, bf16[256,512]{1,0:T(8,128)(2,1)} %k_hbm.1, bf16[256,1024]{1,0:T(8,128)(2,1)} %v_hbm.1, bf16[256,1024]{1,0:T(8,128)(2,1)} %gate_hbm.1, f32[8,256]{1,0:T(8,128)} %bitcast.3, f32[8,256]{1,0:T(8,128)} %bitcast.4, f32[1,128]{1,0:T(1,128)} %bitcast.5, ...), custom_call_target="tpu_custom_call" | custom-call | tf_op jit(solution)/shard_map/pallas_call | solution.py:430
  41.0 1.7 %copy.10 = bf16[64,2048]{1,0:T(8,128)(2,1)} copy(bf16[64,2048]{1,0:T(8,128)(2,1)} %shard_map.82) | data formatting | bytes 524288

commit v8 on v6

--- a/solution.py
+++ b/solution.py
@@ -224,17 +224,20 @@
             map_copy(head, me, head * apart).start()
 
     half = q_ref.shape[0] // 2
-    for head in range(heads):
-        place = slice(head * DV, (head + 1) * DV)
-        group = head // sharing
-        queries = q_ref[:, group * DK : (group + 1) * DK].astype(f32)
-        decayed, query_scale = parts[head][4:6]
-        top = mm(scores_ref[head, :half, :half], both_ref[head, :half])
-        low = mm(scores_ref[head, half:], both_ref[head])
-        seen = jnp.concatenate([top, low], axis=0)
-        read_ref[:, place] = ((decayed * queries - seen[:, :DK]) * query_scale).astype(bf16)
-        own_ref[:, place] = seen[:, DK:] * query_scale
-
+
+    def own_part(chosen):
+        for head in chosen:
+            place = slice(head * DV, (head + 1) * DV)
+            group = head // sharing
+            queries = q_ref[:, group * DK : (group + 1) * DK].astype(f32)
+            decayed, query_scale = parts[head][4:6]
+            top = mm(scores_ref[head, :half, :half], both_ref[head, :half])
+            low = mm(scores_ref[head, half:], both_ref[head])
+            seen = jnp.concatenate([top, low], axis=0)
+            read_ref[:, place] = ((decayed * queries - seen[:, :DK]) * query_scale).astype(bf16)
+            own_ref[:, place] = seen[:, DK:] * query_scale
+
+    own_part(range(heads // 2))
     for load in loads[5:]:
         load.wait()
     gain = gain_ref[...]
@@ -279,6 +282,7 @@
         def _():
             state[pl.ds(my_head, 1)] = leaving[pl.ds(me, 1)]
 
+    own_part(range(heads // 2, heads))
     for head in range(heads):
         @pl.when((me > 0) & (me != head * apart))
         def _():

time: 42.4 us -> 42.4 us (level)
  no operation moved by 1% of the time
where the time goes in v8:
time: 42.4 us; the launch traced here: 42.2 us
  Pallas kernels  40.5 us (96%)
  local copies, waits for them, and re-layouts  1.67 us (4%)
    pallas_call x1, Pallas kernels, local(): pl.pallas_call(functools.partial(layer_kernel, n, groups), in_specs=[pl.B...  40.5 us
    unnamed x1, local copies, waits for them, and re-layouts  1.67 us

profile of v8, /device:TPU:19, one launch (start us, length us, event | category | flops | bytes accessed | tf_op | source)
XLA Modules:
  0.0 42.2 jit_solution(4143230978827139749)
XLA Ops:
  0.0 40.5 %shard_map.82 = bf16[64,2048]{1,0:T(8,128)(2,1)} custom-call(bf16[256,512]{1,0:T(8,128)(2,1)} %q_hbm.1, bf16[256,512]{1,0:T(8,128)(2,1)} %k_hbm.1, bf16[256,1024]{1,0:T(8,128)(2,1)} %v_hbm.1, bf16[256,1024]{1,0:T(8,128)(2,1)} %gate_hbm.1, f32[8,256]{1,0:T(8,128)} %bitcast.3, f32[8,256]{1,0:T(8,128)} %bitcast.4, f32[1,128]{1,0:T(1,128)} %bitcast.5, ...), custom_call_target="tpu_custom_call" | custom-call | tf_op jit(solution)/shard_map/pallas_call | solution.py:437
  40.5 1.7 %copy.10 = bf16[64,2048]{1,0:T(8,128)(2,1)} copy(bf16[64,2048]{1,0:T(8,128)(2,1)} %shard_map.82) | data formatting | bytes 524288
